TPU v7x, 32 devices: a whole 2x2x4 slice. The times are simulated.
32 devices in a mesh: items: 16 (over z, x, core), blk: 2 (over y).
Axes of the slice: x: 2, y: 2, z: 4, core: 2. Of those that a mesh axis runs over, the one named last changes fastest.
Arguments:
- byte_ids: int32 [32, 2048], P('items', 'blk'), may hold values from 0 to 261
- span_start: int32 [32, 8], P('items'), may hold values from 0 to 1920, as said below
- span_len: int32 [32, 8], P('items'), may hold values from 13 to 128, as said below
- embedding: bfloat16 [262, 768], replicated, may hold values from -6 to 6
- position: bfloat16 [2048, 768], replicated, may hold values from -5 to 5
- mask_vector: bfloat16 [768], replicated, may hold values from -6 to 6
- gain_bytes: bfloat16 [768], replicated, may hold values from 0.5 to 1.5
- key_enc: bfloat16 [768, 256], replicated, may hold values from -0.21875 to 0.21875
- value_enc: bfloat16 [768, 1280], replicated, may hold values from -0.21875 to 0.21875
- latent_init: bfloat16 [256, 1280], replicated, may hold values from -6 to 6
- gain_latent: bfloat16 [1280], replicated, may hold values from 0.5 to 1.5
- query_enc: bfloat16 [1280, 256], replicated, may hold values from -0.15625 to 0.15625
- out_enc: bfloat16 [1280, 1280], replicated, may hold values from -0.625 to 0.625
- gain_enc_mlp: bfloat16 [1280], replicated, may hold values from 0.5 to 1.5
- up_enc: bfloat16 [1280, 1280], replicated, may hold values from -0.15625 to 0.15625
- down_enc: bfloat16 [1280, 1280], replicated, may hold values from -0.25 to 0.25
- gain_self: bfloat16 [1280], replicated, may hold values from 0.5 to 1.5
- query_self: bfloat16 [1280, 256], replicated, may hold values from -0.15625 to 0.15625
- key_self: bfloat16 [1280, 256], replicated, may hold values from -0.15625 to 0.15625
- value_self: bfloat16 [1280, 1280], replicated, may hold values from -0.15625 to 0.15625
- out_self: bfloat16 [1280, 1280], replicated, may hold values from -0.5 to 0.5
- gain_self_mlp: bfloat16 [1280], replicated, may hold values from 0.5 to 1.5
- up_self: bfloat16 [1280, 1280], replicated, may hold values from -0.15625 to 0.15625
- down_self: bfloat16 [1280, 1280], replicated, may hold values from -0.25 to 0.25
- gain_dec_kv: bfloat16 [1280], replicated, may hold values from 0.5 to 1.5
- key_dec: bfloat16 [1280, 256], replicated, may hold values from -0.15625 to 0.15625
- value_dec: bfloat16 [1280, 768], replicated, may hold values from -0.15625 to 0.15625
- dec_query: bfloat16 [2048, 768], replicated, may hold values from -6 to 6
- gain_dec_q: bfloat16 [768], replicated, may hold values from 0.5 to 1.5
- query_dec: bfloat16 [768, 256], replicated, may hold values from -0.21875 to 0.21875
- out_dec: bfloat16 [768, 768], replicated, may hold values from -0.625 to 0.625
- gain_final: bfloat16 [768], replicated, may hold values from 0.5 to 1.5
- logit_cot: bfloat16 [32, 2048, 262], P('items', 'blk'), may hold values from -6 to 6
Outputs:
- logits: bfloat16 [32, 2048, 262], P('items', 'blk')
- grad_embedding: float32 [262, 768], P(None, ('items', 'blk'))
- grad_position: float32 [2048, 768], P(('items', 'blk'))
- grad_mask_vector: float32 [768], P(('items', 'blk'))
- grad_gain_bytes: float32 [768], P(('items', 'blk'))
- grad_key_enc: float32 [768, 256], P(('items', 'blk'))
- grad_value_enc: float32 [768, 1280], P(('items', 'blk'))
- grad_latent_init: float32 [256, 1280], P(('items', 'blk'))
- grad_gain_latent: float32 [1280], P(('items', 'blk'))
- grad_query_enc: float32 [1280, 256], P(('items', 'blk'))
- grad_out_enc: float32 [1280, 1280], P(('items', 'blk'))
- grad_gain_enc_mlp: float32 [1280], P(('items', 'blk'))
- grad_up_enc: float32 [1280, 1280], P(('items', 'blk'))
- grad_down_enc: float32 [1280, 1280], P(('items', 'blk'))
- grad_gain_self: float32 [1280], P(('items', 'blk'))
- grad_query_self: float32 [1280, 256], P(('items', 'blk'))
- grad_key_self: float32 [1280, 256], P(('items', 'blk'))
- grad_value_self: float32 [1280, 1280], P(('items', 'blk'))
- grad_out_self: float32 [1280, 1280], P(('items', 'blk'))
- grad_gain_self_mlp: float32 [1280], P(('items', 'blk'))
- grad_up_self: float32 [1280, 1280], P(('items', 'blk'))
- grad_down_self: float32 [1280, 1280], P(('items', 'blk'))
- grad_gain_dec_kv: float32 [1280], P(('items', 'blk'))
- grad_key_dec: float32 [1280, 256], P(('items', 'blk'))
- grad_value_dec: float32 [1280, 768], P(('items', 'blk'))
- grad_dec_query: float32 [2048, 768], P(('items', 'blk'))
- grad_gain_dec_q: float32 [768], P(('items', 'blk'))
- grad_query_dec: float32 [768, 256], P(('items', 'blk'))
- grad_out_dec: float32 [768, 768], P(('items', 'blk'))
- grad_gain_final: float32 [768], P(('items', 'blk'))
Inputs may be any that keep to these rules, and one draw needn't show every extreme that they name: `span_start`: span s of an item lies inside bytes s * 256 to (s + 1) * 256 - 1; all spans of one item have the same length. `span_len`: between 5 and 50 percent of each item's bytes are masked.
All inputs are finite; a program needn't handle non-finite values.
Results may differ from a plain program's by a relative error of at most 0.02.
Values may be sent and summed in bfloat16 or wider, within the bound.
A program may use at most 384 MiB of HBM per device.

v0:
```python
import jax
import jax.numpy as jnp
from jax import lax
from jax.sharding import PartitionSpec as P

HEADS = 8
EPS = 1e-05
F32 = jnp.float32
BF16 = jnp.bfloat16
GELU_C = 0.7978845608028654
GELU_A = 0.044715


def nn(a, b):
    return lax.dot_general(a, b, (((1,), (0,)), ((), ())), preferred_element_type=F32)


def nt(a, b):
    return lax.dot_general(a, b, (((1,), (1,)), ((), ())), preferred_element_type=F32)


def tn(a, b):
    return lax.dot_general(a, b, (((0,), (0,)), ((), ())), preferred_element_type=F32)


def norm_forward(x, gain):
    centered = x - jnp.mean(x, axis=-1, keepdims=True)
    variance = jnp.mean(centered * centered, axis=-1, keepdims=True)
    rstd = lax.rsqrt(variance + EPS)
    hat = centered * rstd
    return (hat * gain.astype(F32)).astype(BF16), hat, rstd


def norm_backward(dy, hat, rstd, gain):
    dgain = jnp.sum(dy * hat, axis=0)
    dhat = dy * gain.astype(F32)
    first = jnp.mean(dhat, axis=-1, keepdims=True)
    second = jnp.mean(dhat * hat, axis=-1, keepdims=True)
    return rstd * (dhat - first - hat * second), dgain


def gelu_forward(u):
    t = jnp.tanh(GELU_C * (u + GELU_A * u * u * u))
    return (0.5 * u * (1.0 + t)).astype(BF16)


def gelu_backward(dh, u):
    t = jnp.tanh(GELU_C * (u + GELU_A * u * u * u))
    slope = 0.5 * (1.0 + t) + 0.5 * u * (1.0 - t * t) * GELU_C * (1.0 + 3.0 * GELU_A * u * u)
    return dh * slope


def softmax(s):
    e = jnp.exp(s - jnp.max(s, axis=-1, keepdims=True))
    return e / jnp.sum(e, axis=-1, keepdims=True)


def softmax_backward(dp, soft, scale):
    inner = jnp.sum(dp * soft, axis=-1, keepdims=True)
    return (soft * (dp - inner) * scale).astype(BF16)


class Reducer:
    def __init__(self):
        n_items = lax.axis_size("items")
        self.count = n_items * lax.axis_size("blk")
        self.k = n_items.bit_length() - 1
        self.n_items = n_items

    def bit(self, name):
        if name == "y":
            return lax.axis_index("blk")
        return (lax.axis_index("items") >> name) & 1

    def exchange(self, x, name):
        if name == "y":
            return lax.ppermute(x, "blk", [(0, 1), (1, 0)])
        return lax.ppermute(x, "items", [(i, i ^ (1 << name)) for i in range(self.n_items)])

    def split(self, g):
        rows, width = g.shape
        return g.astype(BF16).reshape((2,) * (self.k + 1) + (rows // self.count, width))

    def reduce(self, grads, order):
        dims = list(range(self.k - 1, -1, -1)) + ["y"]
        parts = [self.split(g) for g in grads]
        heights = [p.shape[-2] for p in parts]
        for number, name in enumerate(order):
            axis = dims.index(name)
            mine = self.bit(name)
            send = [lax.dynamic_index_in_dim(p, 1 - mine, axis, keepdims=False) for p in parts]
            keep = [lax.dynamic_index_in_dim(p, mine, axis, keepdims=False) for p in parts]
            if number == 0:
                send = [jnp.concatenate(send, axis=-2)] if len(send) > 1 else send
                keep = [jnp.concatenate(keep, axis=-2)] if len(keep) > 1 else keep
            got = self.exchange(send[0], name)
            total = keep[0].astype(F32) + got.astype(F32)
            last = number == len(order) - 1
            parts = [total if last else total.astype(BF16)]
            dims.pop(axis)
        out, at = [], 0
        for height in heights:
            out.append(parts[0][at : at + height])
            at += height
        return out


def local(
    byte_ids, span_start, span_len, embedding, position, mask_vector, gain_bytes, key_enc,
    value_enc, latent_init, gain_latent, query_enc, out_enc, gain_enc_mlp, up_enc, down_enc,
    gain_self, query_self, key_self, value_self, out_self, gain_self_mlp, up_self, down_self,
    gain_dec_kv, key_dec, value_dec, dec_query, gain_dec_q, query_dec, out_dec, gain_final,
    logit_cot,
):
    me = lax.axis_index("blk")
    half = byte_ids.shape[1]
    total = position.shape[0]
    vocab = embedding.shape[0]
    latents = latent_init.shape[0]
    reducer = Reducer()
    k = reducer.k
    order_yx = [0, "y", 1] + list(range(2, k))
    order_xy = [0, 1, "y"] + list(range(2, k))

    def swap(x):
        return lax.ppermute(x, "blk", [(0, 1), (1, 0)])

    def own_item(x):
        mine = lax.dynamic_index_in_dim(x, me, 0, keepdims=False)
        got = swap(lax.dynamic_index_in_dim(x, 1 - me, 0, keepdims=False))
        low_half = jnp.where(me == 0, mine, got)
        high_half = jnp.where(me == 0, got, mine)
        return jnp.concatenate([low_half, high_half], axis=0)

    ids = own_item(byte_ids)
    cot = own_item(logit_cot)
    starts = lax.dynamic_index_in_dim(span_start, me, 0, keepdims=False)
    lengths = lax.dynamic_index_in_dim(span_len, me, 0, keepdims=False)

    places = lax.iota(jnp.int32, total)
    inside = (places[None, :] >= starts[:, None]) & (places[None, :] < (starts + lengths)[:, None])
    codes = jnp.where(jnp.any(inside, axis=0), vocab, ids)
    padded = 512
    table = jnp.concatenate(
        [embedding, mask_vector[None, :], jnp.zeros((padded - vocab - 1, embedding.shape[1]), BF16)], axis=0
    )
    onehot = (codes[:, None] == lax.iota(jnp.int32, padded)[None, :]).astype(BF16)
    bytes_in = nn(onehot, table) + position.astype(F32)
    nb, hat_b, rstd_b = norm_forward(bytes_in, gain_bytes)
    k_e = nn(nb, key_enc).astype(BF16)
    v_e = nn(nb, value_enc).astype(BF16)

    latent32 = latent_init.astype(F32)
    nl, hat_l, rstd_l = norm_forward(latent32, gain_latent)
    q_e = nn(nl, query_enc).astype(BF16)
    scale_e = q_e.shape[1] ** (-0.5)
    soft_e = softmax(nt(q_e, k_e) * scale_e)
    p_e = soft_e.astype(BF16)
    a_e = nn(p_e, v_e).astype(BF16)
    after_enc = latent32 + nn(a_e, out_enc)
    n1, hat1, rstd1 = norm_forward(after_enc, gain_enc_mlp)
    u1 = nn(n1, up_enc)
    h1 = gelu_forward(u1)
    encoded = after_enc + nn(h1, down_enc)
    n2, hat2, rstd2 = norm_forward(encoded, gain_self)
    q_s = nn(n2, query_self).astype(BF16)
    k_s = nn(n2, key_self).astype(BF16)
    v_s = nn(n2, value_self).astype(BF16)

    def heads(x):
        return x.reshape(latents, HEADS, -1).transpose(1, 0, 2)

    def bdot(a, b, ca, cb):
        return lax.dot_general(a, b, (((ca,), (cb,)), ((0,), (0,))), preferred_element_type=F32)

    qh, kh, vh = heads(q_s), heads(k_s), heads(v_s)
    scale_s = qh.shape[2] ** (-0.5)
    soft_s = softmax(bdot(qh, kh, 2, 2) * scale_s)
    p_s = soft_s.astype(BF16)
    ah = bdot(p_s, vh, 2, 1).astype(BF16)
    a_s = ah.transpose(1, 0, 2).reshape(latents, -1)
    after_self = encoded + nn(a_s, out_self)
    n3, hat3, rstd3 = norm_forward(after_self, gain_self_mlp)
    u2 = nn(n3, up_self)
    h2 = gelu_forward(u2)
    latent_out = after_self + nn(h2, down_self)
    n4, hat4, rstd4 = norm_forward(latent_out, gain_dec_kv)
    k_d = nn(n4, key_dec).astype(BF16)
    v_d = nn(n4, value_dec).astype(BF16)

    query32 = dec_query.astype(F32)
    nq, hat_q, rstd_q = norm_forward(query32, gain_dec_q)
    q_d = nn(nq, query_dec).astype(BF16)
    scale_d = q_d.shape[1] ** (-0.5)
    soft_d = softmax(nt(q_d, k_d) * scale_d)
    p_d = soft_d.astype(BF16)
    a_d = nn(p_d, v_d).astype(BF16)
    decoded = query32 + nn(a_d, out_dec)
    nf, hat_f, rstd_f = norm_forward(decoded, gain_final)
    logits = nt(nf, embedding).astype(BF16)

    low_rows, high_rows = logits[:half], logits[half:]
    mine = jnp.where(me == 0, low_rows, high_rows)
    got = swap(jnp.where(me == 0, high_rows, low_rows))
    logits_out = jnp.stack([jnp.where(me == 0, mine, got), jnp.where(me == 0, got, mine)])

    dnf = nn(cot, embedding)
    g_emb_out = tn(nf, cot)
    ddec, g_gain_final = norm_backward(dnf, hat_f, rstd_f, gain_final)
    ddec16 = ddec.astype(BF16)
    da_d = nt(ddec16, out_dec)
    g_out_dec = tn(a_d, ddec16)
    da16 = da_d.astype(BF16)
    dv_d = tn(p_d, da16).astype(BF16)
    dp = nt(da16, v_d)
    ds = softmax_backward(dp, soft_d, scale_d)
    dq_d = nn(ds, k_d).astype(BF16)
    dk_d = tn(ds, q_d).astype(BF16)
    g_query_dec = tn(nq, dq_d)
    dnq, g_gain_dec_q = norm_backward(nt(dq_d, query_dec), hat_q, rstd_q, gain_dec_q)
    g_dec_query = ddec + dnq

    g_key_dec = tn(n4, dk_d)
    g_value_dec = tn(n4, dv_d)
    dlat, g_gain_dec_kv = norm_backward(nt(dk_d, key_dec) + nt(dv_d, value_dec), hat4, rstd4, gain_dec_kv)
    dlat16 = dlat.astype(BF16)
    g_down_self = tn(h2, dlat16)
    du2 = gelu_backward(nt(dlat16, down_self), u2).astype(BF16)
    g_up_self = tn(n3, du2)
    dx3, g_gain_self_mlp = norm_backward(nt(du2, up_self), hat3, rstd3, gain_self_mlp)
    dafter_self = dlat + dx3
    das16 = dafter_self.astype(BF16)
    g_out_self = tn(a_s, das16)
    da_s = heads(nt(das16, out_self))
    dah16 = da_s.astype(BF16)
    dvh = bdot(p_s, dah16, 1, 1)
    dps = bdot(dah16, vh, 2, 2)
    dss = softmax_backward(dps, soft_s, scale_s)
    dqh = bdot(dss, kh, 2, 1)
    dkh = bdot(dss, qh, 1, 1)

    def unheads(x):
        return x.transpose(1, 0, 2).reshape(latents, -1).astype(BF16)

    dq_s, dk_s, dv_s = unheads(dqh), unheads(dkh), unheads(dvh)
    g_query_self = tn(n2, dq_s)
    g_key_self = tn(n2, dk_s)
    g_value_self = tn(n2, dv_s)
    dn2 = nt(dq_s, query_self) + nt(dk_s, key_self) + nt(dv_s, value_self)
    dx2, g_gain_self = norm_backward(dn2, hat2, rstd2, gain_self)
    denc = dafter_self + dx2
    denc16 = denc.astype(BF16)
    g_down_enc = tn(h1, denc16)
    du1 = gelu_backward(nt(denc16, down_enc), u1).astype(BF16)
    g_up_enc = tn(n1, du1)
    dx1, g_gain_enc_mlp = norm_backward(nt(du1, up_enc), hat1, rstd1, gain_enc_mlp)
    dafter = denc + dx1
    daft16 = dafter.astype(BF16)
    g_out_enc = tn(a_e, daft16)
    da_e = nt(daft16, out_enc)
    dae16 = da_e.astype(BF16)
    dv_e = tn(p_e, dae16).astype(BF16)
    dpe = nt(dae16, v_e)
    dse = softmax_backward(dpe, soft_e, scale_e)
    dq_e = nn(dse, k_e).astype(BF16)
    dk_e = tn(dse, q_e).astype(BF16)
    g_query_enc = tn(nl, dq_e)
    dxl, g_gain_latent = norm_backward(nt(dq_e, query_enc), hat_l, rstd_l, gain_latent)
    g_latent = dafter + dxl

    g_key_enc = tn(nb, dk_e)
    g_value_enc = tn(nb, dv_e)
    dnb = nt(dk_e, key_enc) + nt(dv_e, value_enc)
    dbytes, g_gain_bytes = norm_backward(dnb, hat_b, rstd_b, gain_bytes)
    g_table = tn(dbytes.astype(BF16), onehot)
    g_emb = jnp.concatenate(
        [
            g_table[:, :vocab] + g_emb_out,
            g_table[:, vocab : vocab + 1],
            g_gain_bytes[:, None],
            g_gain_dec_q[:, None],
            g_gain_final[:, None],
            jnp.zeros((g_table.shape[0], padded - vocab - 4), F32),
        ],
        axis=1,
    )
    g_gains = jnp.stack(
        [g_gain_latent, g_gain_enc_mlp, g_gain_self, g_gain_self_mlp, g_gain_dec_kv], axis=1
    )
    g_gains = jnp.pad(g_gains, ((0, 0), (0, 256 - 5)))

    r_dec_query, r_out_dec, r_value_dec = reducer.reduce([g_dec_query, g_out_dec, g_value_dec], order_yx)
    r_down_self, r_up_self, r_out_self = reducer.reduce([g_down_self, g_up_self, g_out_self], order_xy)
    r_value_self, r_down_enc = reducer.reduce([g_value_self, g_down_enc], order_yx)
    r_up_enc, r_out_enc = reducer.reduce([g_up_enc, g_out_enc], order_xy)
    r_query_dec, r_key_dec, r_query_self, r_key_self = reducer.reduce(
        [g_query_dec, g_key_dec, g_query_self, g_key_self], order_xy
    )
    r_value_enc, r_latent = reducer.reduce([g_value_enc, g_latent], order_xy)
    (r_position,) = reducer.reduce([dbytes], order_yx)
    r_key_enc, r_query_enc, r_gains, r_emb_a, r_emb_b = reducer.reduce(
        [g_key_enc, g_query_enc, g_gains, g_emb[:, :256], g_emb[:, 256:]], order_yx
    )
    r_emb = jnp.concatenate([r_emb_a, r_emb_b], axis=1)
    return (
        logits_out,
        r_emb[:, :vocab].T,
        r_position,
        r_emb[:, vocab],
        r_emb[:, vocab + 1],
        r_key_enc,
        r_value_enc,
        r_latent,
        r_gains[:, 0],
        r_query_enc,
        r_out_enc,
        r_gains[:, 1],
        r_up_enc,
        r_down_enc,
        r_gains[:, 2],
        r_query_self,
        r_key_self,
        r_value_self,
        r_out_self,
        r_gains[:, 3],
        r_up_self,
        r_down_self,
        r_gains[:, 4],
        r_key_dec,
        r_value_dec,
        r_dec_query,
        r_emb[:, vocab + 2],
        r_query_dec,
        r_out_dec,
        r_emb[:, vocab + 3],
    )


def solution(mesh):
    split = P("items", "blk")
    rows = P(("items", "blk"))
    outs = [P("items", "blk", None), P(None, ("items", "blk"))] + [rows] * 28
    return jax.shard_map(
        local,
        mesh=mesh,
        in_specs=(split, P("items", None), P("items", None)) + (P(),) * 29 + (P("items", "blk", None),),
        out_specs=tuple(outs),
        check_vma=False,
    )
```

profile of v0, /device:TPU:0, one launch (start us, length us, event | category | flops | bytes accessed | tf_op | source)
XLA Modules:
  0.0 622.9 jit_solution(4692876279836463434)
XLA Ops:
  1.6 3.0 collective-permute-start
  4.6 4.9 constant_dynamic-slice_fusion.35
  17.2 4.4 fusion.166
  28.0 6.7 %fusion.175 = f32[2048,1280]{1,0:T(8,128)} fusion(bf16[2048,768]{1,0:T(8,128)(2,1)S(1)} %multiply_convert_fusion.2, bf16[768,1280]{1,0:T(8,128)(2,1)S(1)} %copy-done.190), kind=kOutput, calls=%fused_computation.481 | convolution fusion | flops 4026531840 | bytes 15597568 | tf_op jit(solution)/shard_map/dot_general | solution.py:15
  36.5 7.2 %online-softmax = f32[256,1280]{1,0:T(8,128)} custom-call(f32[256,2048]{1,0:T(8,128)} %get-tuple-element.278, f32[2048,1280]{1,0:T(8,128)} %fusion.175), custom_call_target="tpu_custom_call" | custom-call | tf_op online-softmax
  43.7 3.7 fusion.167
  55.7 2.2 copy.217
  60.8 3.1 fusion.169
  63.9 3.1 convolution_convert_fusion.23
  67.1 3.6 fusion.170
  80.1 5.6 online-softmax.1
  85.8 7.1 %fusion.172 = (f32[2048]{0:T(1024)S(1)}, f32[2048,768]{1,0:T(8,128)S(1)}) fusion(bf16[768,768]{1,0:T(8,128)(2,1)} %param.63, f32[2048,768]{1,0:T(8,128)} %online-softmax.1, bf16[2048,768]{1,0:T(8,128)(2,1)} %param.60), kind=kOutput, calls=%fused_computation.478 | convolution fusion | flops 2422208512 | bytes 16916480 | tf_op jit(solution)/shard_map/dot_general | solution.py:15
  97.6 3.9 multiply_reduce_fusion
  101.5 3.7 subtract_multiply_fusion
  105.2 2.9 convolution_convert_fusion.9
  126.0 2.2 convolution_convert_fusion.24
  130.0 5.1 fusion.88
  135.1 5.0 fusion.91
  140.1 3.1 fusion.180
  161.4 2.2 fusion.67
  166.7 2.6 copy-done.72
  171.2 4.6 fusion.181
  175.9 3.5 multiply_reduce_fusion.1
  181.5 2.2 fusion.19
  186.0 8.5 %convolution_convert_fusion.10 = bf16[768,1280]{1,0:T(8,128)(2,1)} fusion(bf16[2048,768]{1,0:T(8,128)(2,1)S(1)} %copy-done.72, bf16[2048,1280]{1,0:T(8,128)(2,1)} %copy-done.205), kind=kOutput, calls=%fused_computation.58 | convolution fusion | flops 4027514880 | bytes 10354688 | tf_op jit(solution)/shard_map/dot_general | solution.py:23
  194.5 2.7 convolution_convert_fusion.5
  197.3 2.8 convolution_convert_fusion.6
  200.1 3.1 convolution_convert_fusion.3
  203.3 2.7 convolution_convert_fusion.4
  209.8 4.5 fusion.10
  216.1 2.8 convolution_convert_fusion
  219.0 3.0 convolution_convert_fusion.1
  222.0 3.1 convolution_convert_fusion.2
  227.1 3.8 fusion.60
  241.2 8.5 %concatenate.65 = bf16[768,512]{0,1:T(8,128)(2,1)} concatenate(bf16[768,262]{0,1:T(8,128)(2,1)} %fusion.84, bf16[768,1]{0,1:T(2,128)(2,1)S(1)} %slice.215, bf16[768,1]{0,1:T(2,128)(2,1)S(1)} %broadcast_in_dim.22, bf16[768,1]{0,1:T(2,128)(2,1)S(1)} %broadcast_in_dim.23, bf16[768,1]{0,1:T(2,128)(2,1)S(1)} %broadcast_in_dim.24, bf16[768,246]{0,1:T(8,128)(2,1)} %broadcast_in_dim.25), dimensions={1} | concatenate | bytes 1572864 | tf_op jit(solution)/shard_map/concatenate | solution.py:276
  297.6 4.8 fusion.14
  305.1 2.4 pad_maximum_fusion
  334.3 9.4 %collective-permute-done.29 = bf16[2,2,2,144,256]{4,3,0,1,2:T(8,128)(2,1)S(1)} collective-permute-done((bf16[2,2,2,144,256]{4,3,0,1,2:T(8,128)(2,1)S(1)}, bf16[2,2,2,144,256]{4,3,0,1,2:T(8,128)(2,1)S(1)}, u32[]{:S(2)}, u32[]{:S(2)}) %collective-permute-start.29) | collective-permute-done | bytes 589856 | tf_op jit(solution)/shard_map/ppermute | solution.py:78
  348.2 11.3 %collective-permute-done.14 = bf16[2,2,2,32,1280]{4,3,0,1,2:T(8,128)(2,1)S(1)} collective-permute-done((bf16[2,2,2,32,1280]{4,3,0,1,2:T(8,128)(2,1)S(1)}, bf16[2,2,2,32,1280]{4,3,0,1,2:T(8,128)(2,1)S(1)}, u32[]{:S(2)}, u32[]{:S(2)}) %collective-permute-start.14) | collective-permute-done | bytes 655392 | tf_op jit(solution)/shard_map/ppermute | solution.py:78
  360.2 12.0 %collective-permute-done.30 = bf16[2,2,144,256]{3,2,0,1:T(8,128)(2,1)S(1)} collective-permute-done((bf16[2,2,144,256]{3,2,0,1:T(8,128)(2,1)S(1)}, bf16[2,2,144,256]{3,2,0,1:T(8,128)(2,1)S(1)}, u32[]{:S(2)}, u32[]{:S(2)}) %collective-permute-start.30) | collective-permute-done | bytes 294944 | tf_op jit(solution)/shard_map/ppermute | solution.py:77
  372.8 6.6 %collective-permute-done.5 = bf16[2,2,152,256]{3,2,1,0:T(8,128)(2,1)S(1)} collective-permute-done((bf16[2,2,152,256]{3,2,1,0:T(8,128)(2,1)S(1)}, bf16[2,2,152,256]{3,2,1,0:T(8,128)(2,1)S(1)}, u32[]{:S(2)}, u32[]{:S(2)}) %collective-permute-start.5) | collective-permute-done | bytes 311328 | tf_op jit(solution)/shard_map/ppermute | solution.py:78
  381.0 4.3 collective-permute-done.31
  385.4 2.7 collective-permute-start.32
  388.0 3.4 collective-permute-done.32
  393.3 5.3 collective-permute-done.15
  399.1 4.7 collective-permute-done.6
  406.1 5.2 collective-permute-done.7
  414.7 2.4 collective-permute-done.16
  417.7 9.3 %collective-permute-done.10 = bf16[2,2,64,768]{3,2,0,1:T(8,128)(2,1)S(1)} collective-permute-done((bf16[2,2,64,768]{3,2,0,1:T(8,128)(2,1)S(1)}, bf16[2,2,64,768]{3,2,0,1:T(8,128)(2,1)S(1)}, u32[]{:S(2)}, u32[]{:S(2)}) %collective-permute-start.10) | collective-permute-done | bytes 393248 | tf_op jit(solution)/shard_map/ppermute | solution.py:78
  427.9 5.0 collective-permute-done.11
  432.8 3.2 collective-permute-start.17
  440.7 2.7 add_convert_fusion.1
  447.1 29.2 %collective-permute-done.39 = bf16[2,2,2,128,768]{4,3,0,1,2:T(8,128)(2,1)} collective-permute-done((bf16[2,2,2,128,768]{4,3,0,1,2:T(8,128)(2,1)}, bf16[2,2,2,128,768]{4,3,0,1,2:T(8,128)(2,1)}, u32[]{:S(2)}, u32[]{:S(2)}) %collective-permute-start.39) | collective-permute-done | bytes 1572896 | tf_op jit(solution)/shard_map/ppermute | solution.py:77
  480.6 30.6 %collective-permute-done.24 = bf16[2,2,2,80,1280]{4,3,0,1,2:T(8,128)(2,1)S(1)} collective-permute-done((bf16[2,2,2,80,1280]{4,3,0,1,2:T(8,128)(2,1)S(1)}, bf16[2,2,2,80,1280]{4,3,0,1,2:T(8,128)(2,1)S(1)}, u32[]{:S(2)}, u32[]{:S(2)}) %collective-permute-start.24) | collective-permute-done | bytes 1638432 | tf_op jit(solution)/shard_map/ppermute | solution.py:77
  516.5 8.0 %collective-permute-done.20 = bf16[2,2,80,1280]{3,2,0,1:T(8,128)(2,1)S(1)} collective-permute-done((bf16[2,2,80,1280]{3,2,0,1:T(8,128)(2,1)S(1)}, bf16[2,2,80,1280]{3,2,0,1:T(8,128)(2,1)S(1)}, u32[]{:S(2)}, u32[]{:S(2)}) %collective-permute-start.20) | collective-permute-done | bytes 819232 | tf_op jit(solution)/shard_map/ppermute | solution.py:77
  525.9 7.1 %collective-permute-done.25 = bf16[2,2,80,1280]{3,2,0,1:T(8,128)(2,1)S(1)} collective-permute-done((bf16[2,2,80,1280]{3,2,0,1:T(8,128)(2,1)S(1)}, bf16[2,2,80,1280]{3,2,0,1:T(8,128)(2,1)S(1)}, u32[]{:S(2)}, u32[]{:S(2)}) %collective-permute-start.25) | collective-permute-done | bytes 819232 | tf_op jit(solution)/shard_map/ppermute | solution.py:78
  533.3 3.0 collective-permute-start.42
  537.3 3.4 collective-permute-done.42
  542.9 33.2 %collective-permute-done.34 = bf16[2,2,2,120,1280]{4,3,0,1,2:T(8,128)(2,1)S(1)} collective-permute-done((bf16[2,2,2,120,1280]{4,3,0,1,2:T(8,128)(2,1)S(1)}, bf16[2,2,2,120,1280]{4,3,0,1,2:T(8,128)(2,1)S(1)}, u32[]{:S(2)}, u32[]{:S(2)}) %collective-permute-start.34) | collective-permute-done | bytes 2457632 | tf_op jit(solution)/shard_map/ppermute | solution.py:78
  577.3 2.4 collective-permute-start.22
  580.5 7.9 %collective-permute-done.22 = bf16[80,1280]{1,0:T(8,128)(2,1)S(1)} collective-permute-done((bf16[80,1280]{1,0:T(8,128)(2,1)S(1)}, bf16[80,1280]{1,0:T(8,128)(2,1)S(1)}, u32[]{:S(2)}, u32[]{:S(2)}) %collective-permute-start.22) | collective-permute-done | bytes 204832 | tf_op jit(solution)/shard_map/ppermute | solution.py:78
  588.5 7.8 %collective-permute-done.35 = bf16[2,2,120,1280]{3,2,0,1:T(8,128)(2,1)S(1)} collective-permute-done((bf16[2,2,120,1280]{3,2,0,1:T(8,128)(2,1)S(1)}, bf16[2,2,120,1280]{3,2,0,1:T(8,128)(2,1)S(1)}, u32[]{:S(2)}, u32[]{:S(2)}) %collective-permute-start.35) | collective-permute-done | bytes 1228832 | tf_op jit(solution)/shard_map/ppermute | solution.py:77
  599.1 11.0 %collective-permute-done.36 = bf16[2,120,1280]{2,1,0:T(8,128)(2,1)S(1)} collective-permute-done((bf16[2,120,1280]{2,1,0:T(8,128)(2,1)S(1)}, bf16[2,120,1280]{2,1,0:T(8,128)(2,1)S(1)}, u32[]{:S(2)}, u32[]{:S(2)}) %collective-permute-start.36) | collective-permute-done | bytes 614432 | tf_op jit(solution)/shard_map/ppermute | solution.py:78
  612.7 8.8 %collective-permute-done.37 = bf16[120,1280]{1,0:T(8,128)(2,1)S(1)} collective-permute-done((bf16[120,1280]{1,0:T(8,128)(2,1)S(1)}, bf16[120,1280]{1,0:T(8,128)(2,1)S(1)}, u32[]{:S(2)}, u32[]{:S(2)}) %collective-permute-start.37) | collective-permute-done | bytes 307232 | tf_op jit(solution)/shard_map/ppermute | solution.py:78
  (784 shorter events, 230.5 us)
Async XLA Ops:
  0.7 70.3 %copy-start = (bf16[1280,1280]{1,0:T(8,128)(2,1)S(1)}, bf16[1280,1280]{1,0:T(8,128)(2,1)}, u32[]{:S(2)}) copy-start(bf16[1280,1280]{1,0:T(8,128)(2,1)} %param.55) | copy-start | bytes 9830404
  1.6 8.9 %copy-start.174 = (bf16[768]{0:T(1024)(128)(2,1)S(1)}, bf16[768]{0:T(1024)(128)(2,1)}, u32[]{:S(2)}) copy-start(bf16[768]{0:T(1024)(128)(2,1)} %param.61) | copy-start | bytes 4612
  1.6 15.6 %collective-permute-start = (s32[1024]{0:T(1024)S(1)}, s32[1024]{0:T(1024)S(1)}, u32[]{:S(2)}, u32[]{:S(2)}) collective-permute-start(s32[1024]{0:T(1024)S(1)} %bitcast.544), channel_id=1, source_target_pairs={{0,1},{1,0},{2,3},{3,2},{4,5},{5,4},{6,7},{7,6},{8,9},{9,8},{10,11... | collective-permute-start | bytes 12296 | tf_op jit(solution)/shard_map/ppermute | solution.py:126
  10.5 85.5 %collective-permute-start.2 = (bf16[1024,262]{0,1:T(8,128)(2,1)}, bf16[1024,262]{0,1:T(8,128)(2,1)}, u32[]{:S(2)}, u32[]{:S(2)}) collective-permute-start(bf16[1024,262]{0,1:T(8,128)(2,1)} %bitcast.448), channel_id=1, source_target_pairs={{0,1},{1,0},{2,3},{3,2},{4,5},{5,4},{6,7},{7,6},{8,9},{9,8},{10,11... | collective-permute-start | bytes 1609736 | tf_op jit(solution)/shard_map/ppermute | solution.py:126
  16.7 18.0 %copy-start.109 = (bf16[256,256]{1,0:T(8,128)(2,1)}, bf16[256,256]{1,0:T(8,128)(2,1)S(1)}, u32[]{:S(2)}) copy-start(bf16[256,256]{1,0:T(8,128)(2,1)S(1)} %convolution_convert_fusion.31) | copy-start | bytes 393220
  16.9 30.8 %copy-start.129 = (f32[1280]{0:T(1024)}, f32[1280]{0:T(1024)S(1)}, u32[]{:S(2)}) copy-start(f32[1280]{0:T(1024)S(1)} %convert_element_type.727) | copy-start | bytes 15364
  17.0 54.0 %copy-start.126 = (f32[1280]{0:T(1024)}, f32[1280]{0:T(1024)S(1)}, u32[]{:S(2)}) copy-start(f32[1280]{0:T(1024)S(1)} %convert_element_type.738) | copy-start | bytes 15364
  17.0 57.8 %copy-start.118 = (f32[1280]{0:T(1024)}, f32[1280]{0:T(1024)S(1)}, u32[]{:S(2)}) copy-start(f32[1280]{0:T(1024)S(1)} %convert_element_type.741) | copy-start | bytes 15364
  28.0 6.7 %copy-start.60 = (bf16[2048,256]{1,0:T(8,128)(2,1)}, bf16[2048,256]{1,0:T(8,128)(2,1)S(1)}, u32[]{:S(2)}) copy-start(bf16[2048,256]{1,0:T(8,128)(2,1)S(1)} %convolution_convert_fusion.21) | copy-start | bytes 3145732
  36.5 56.4 %copy-start.151 = (f32[256]{0:T(256)}, f32[256]{0:T(256)S(1)}, u32[]{:S(2)}) copy-start(f32[256]{0:T(256)S(1)} %get-tuple-element.277) | copy-start | bytes 3076
  85.8 7.1 %copy-start.3 = (f32[256,2048]{1,0:T(8,128)S(1)}, f32[256,2048]{1,0:T(8,128)}, u32[]{:S(2)}) copy-start(f32[256,2048]{1,0:T(8,128)} %get-tuple-element.278) | copy-start | bytes 6291460
  124.6 21.0 %copy-start.33 = (f32[256,1280]{1,0:T(8,128)}, f32[256,1280]{1,0:T(8,128)S(1)}, u32[]{:S(2)}) copy-start(f32[256,1280]{1,0:T(8,128)S(1)} %multiply_add_fusion.4) | copy-start | bytes 3932164
  128.2 11.9 %copy-start.103 = (bf16[8,256,160]{1,2,0:T(8,128)(2,1)}, bf16[8,256,160]{1,2,0:T(8,128)(2,1)S(1)}, u32[]{:S(2)}) copy-start(bf16[8,256,160]{1,2,0:T(8,128)(2,1)S(1)} %convolution_convert_fusion.24) | copy-start | bytes 1966084
  152.6 42.0 %copy-start.30 = (f32[256,1280]{1,0:T(8,128)}, f32[256,1280]{1,0:T(8,128)S(1)}, u32[]{:S(2)}) copy-start(f32[256,1280]{1,0:T(8,128)S(1)} %multiply_add_fusion.2) | copy-start | bytes 3932164
  169.3 61.6 %copy-start.55 = (bf16[2048,262]{0,1:T(8,128)(2,1)}, bf16[2048,262]{0,1:T(8,128)(2,1)S(1)}, u32[]{:S(2)}) copy-start(bf16[2048,262]{0,1:T(8,128)(2,1)S(1)} %convolution_convert_fusion.11) | copy-start | bytes 3219460
  169.3 6.5 %slice-start = ((s8[6291456]{0:T(1024)(128)(4,1)}), s8[4194304]{0:T(1024)(128)(4,1)S(1)}, s32[]{:S(2)}) async-start(s8[6291456]{0:T(1024)(128)(4,1)} %bitcast.459), calls=%async_computation | async-start | bytes 8388608
  186.0 8.5 %copy-start.32 = (f32[256,1280]{1,0:T(8,128)S(1)}, f32[256,1280]{1,0:T(8,128)}, u32[]{:S(2)}) copy-start(f32[256,1280]{1,0:T(8,128)} %online-softmax) | copy-start | bytes 3932164
  216.1 11.0 %slice-start.9 = ((s8[6291456]{0:T(1024)(128)(4,1)}), s8[4194304]{0:T(1024)(128)(4,1)S(1)}, s32[]{:S(2)}) async-start(s8[6291456]{0:T(1024)(128)(4,1)} %bitcast.489), calls=%async_computation.9 | async-start | bytes 8388608
  219.0 8.1 %slice-start.5 = ((s8[6291456]{0:T(1024)(128)(4,1)}), s8[4194304]{0:T(1024)(128)(4,1)S(1)}, s32[]{:S(2)}) async-start(s8[6291456]{0:T(1024)(128)(4,1)} %bitcast.465), calls=%async_computation.5 | async-start | bytes 8388608
  219.0 8.1 %slice-start.10 = ((s8[6291456]{0:T(1024)(128)(4,1)}), s8[2097152]{0:T(1024)(128)(4,1)S(1)}, s32[]{:S(2)}) async-start(s8[6291456]{0:T(1024)(128)(4,1)} %bitcast.489), calls=%async_computation.10 | async-start | bytes 4194304
  231.8 8.6 %copy-start.162 = (bf16[768]{0:T(1024)(128)(2,1)S(1)}, bf16[768]{0:T(1024)(128)(2,1)}, u32[]{:S(2)}) copy-start(bf16[768]{0:T(1024)(128)(2,1)} %get-tuple-element.152) | copy-start | bytes 4612
  231.8 8.6 %copy-start.178 = (bf16[768]{0:T(1024)(128)(2,1)S(1)}, bf16[768]{0:T(1024)(128)(2,1)}, u32[]{:S(2)}) copy-start(bf16[768]{0:T(1024)(128)(2,1)} %get-tuple-element.150) | copy-start | bytes 4612
  231.8 88.5 %collective-permute-start.1 = (bf16[1024,262]{0,1:T(8,128)(2,1)}, bf16[1024,262]{0,1:T(8,128)(2,1)}, u32[]{:S(2)}, u32[]{:S(2)}) collective-permute-start(bf16[1024,262]{0,1:T(8,128)(2,1)} %broadcast_select_fusion.2), channel_id=1, source_target_pairs={{0,1},{1,0},{2,3},{3,2},{4,5},{5,4},{6,7},{7,6},{8,9},{9,8},{10,11... | collective-permute-start | bytes 1609736 | tf_op jit(solution)/shard_map/ppermute | solution.py:126
  259.5 66.6 %collective-permute-start.3 = (bf16[2,2,2,2,152,256]{5,4,3,2,1,0:T(8,128)(2,1)}, bf16[2,2,2,2,152,256]{5,4,3,2,1,0:T(8,128)(2,1)}, u32[]{:S(2)}, u32[]{:S(2)}) collective-permute-start(bf16[2,2,2,2,152,256]{5,4,3,2,1,0:T(8,128)(2,1)} %get-tuple-element.239), channel_id=1, source_target_pairs={{0,2},{2,0},{4,6},{6,4},{8,10},{10,8},{12,14},{14,12},{16,18},{18,... | collective-permute-start | bytes 3735560 | tf_op jit(solution)/shard_map/ppermute | solution.py:78
  263.3 68.5 %collective-permute-start.8 = (bf16[2,2,2,2,64,768]{5,4,0,1,2,3:T(8,128)(2,1)}, bf16[2,2,2,2,64,768]{5,4,0,1,2,3:T(8,128)(2,1)}, u32[]{:S(2)}, u32[]{:S(2)}) collective-permute-start(bf16[2,2,2,2,64,768]{5,4,0,1,2,3:T(8,128)(2,1)} %bitcast.441), channel_id=1, source_target_pairs={{0,2},{2,0},{4,6},{6,4},{8,10},{10,8},{12,14},{14,12},{16,18},{18,... | collective-permute-start | bytes 4718600 | tf_op jit(solution)/shard_map/ppermute | solution.py:78
  268.6 59.8 %collective-permute-start.13 = (bf16[2,2,2,2,32,1280]{5,4,0,1,3,2:T(8,128)(2,1)}, bf16[2,2,2,2,32,1280]{5,4,0,1,3,2:T(8,128)(2,1)}, u32[]{:S(2)}, u32[]{:S(2)}) collective-permute-start(bf16[2,2,2,2,32,1280]{5,4,0,1,3,2:T(8,128)(2,1)} %pad_maximum_fusion.4), channel_id=1, source_target_pairs={{0,2},{2,0},{4,6},{6,4},{8,10},{10,8},{12,14},{14,12},{16,18},{18,... | collective-permute-start | bytes 3932168 | tf_op jit(solution)/shard_map/ppermute | solution.py:78
  283.8 40.6 %collective-permute-start.28 = (bf16[2,2,2,2,144,256]{5,4,0,1,3,2:T(8,128)(2,1)}, bf16[2,2,2,2,144,256]{5,4,0,1,3,2:T(8,128)(2,1)}, u32[]{:S(2)}, u32[]{:S(2)}) collective-permute-start(bf16[2,2,2,2,144,256]{5,4,0,1,3,2:T(8,128)(2,1)} %pad_maximum_fusion.5), channel_id=1, source_target_pairs={{0,2},{2,0},{4,6},{6,4},{8,10},{10,8},{12,14},{14,12},{16,18},{18,... | collective-permute-start | bytes 3538952 | tf_op jit(solution)/shard_map/ppermute | solution.py:78
  320.4 118.2 %collective-permute-start.18 = (bf16[2,2,2,2,80,1280]{5,4,0,1,3,2:T(8,128)(2,1)S(1)}, bf16[2,2,2,2,80,1280]{5,4,0,1,3,2:T(8,128)(2,1)S(1)}, u32[]{:S(2)}, u32[]{:S(2)}) collective-permute-start(bf16[2,2,2,2,80,1280]{5,4,0,1,3,2:T(8,128)(2,1)S(1)} %pad_maximum_fusion.1), channel_id=1, source_target_pairs={{0,2},{2,0},{4,6},{6,4},{8,10},{10,8},{12,14},{14,12},{16,18},{18,... | collective-permute-start | bytes 9830408 | tf_op jit(solution)/shard_map/ppermute | solution.py:78
  324.4 115.6 %collective-permute-start.23 = (bf16[2,2,2,2,80,1280]{5,4,0,1,2,3:T(8,128)(2,1)}, bf16[2,2,2,2,80,1280]{5,4,0,1,2,3:T(8,128)(2,1)}, u32[]{:S(2)}, u32[]{:S(2)}) collective-permute-start(bf16[2,2,2,2,80,1280]{5,4,0,1,2,3:T(8,128)(2,1)} %pad_maximum_fusion.2), channel_id=1, source_target_pairs={{0,2},{2,0},{4,6},{6,4},{8,10},{10,8},{12,14},{14,12},{16,18},{18,... | collective-permute-start | bytes 9830408 | tf_op jit(solution)/shard_map/ppermute | solution.py:78
  326.2 109.9 %collective-permute-start.38 = (bf16[2,2,2,2,128,768]{5,4,0,1,2,3:T(8,128)(2,1)S(1)}, bf16[2,2,2,2,128,768]{5,4,0,1,2,3:T(8,128)(2,1)S(1)}, u32[]{:S(2)}, u32[]{:S(2)}) collective-permute-start(bf16[2,2,2,2,128,768]{5,4,0,1,2,3:T(8,128)(2,1)S(1)} %pad_maximum_fusion.3), channel_id=1, source_target_pairs={{0,2},{2,0},{4,6},{6,4},{8,10},{10,8},{12,14},{14,12},{16,18},{18,... | collective-permute-start | bytes 9437192 | tf_op jit(solution)/shard_map/ppermute | solution.py:78
  328.4 15.3 %collective-permute-start.29 = (bf16[2,2,2,144,256]{4,3,0,1,2:T(8,128)(2,1)S(1)}, bf16[2,2,2,144,256]{4,3,0,1,2:T(8,128)(2,1)S(1)}, u32[]{:S(2)}, u32[]{:S(2)}) collective-permute-start(bf16[2,2,2,144,256]{4,3,0,1,2:T(8,128)(2,1)S(1)} %dynamic-slice_bitcast_fusion.12), channel_id=1, source_target_pairs={{0,4},{2,6},{4,0},{6,2},{8,12},{10,14},{12,8},{14,10},{16,20},{18,... | collective-permute-start | bytes 1769480 | tf_op jit(solution)/shard_map/ppermute | solution.py:78
  331.8 15.7 %collective-permute-start.4 = (bf16[2,2,2,152,256]{4,3,2,1,0:T(8,128)(2,1)S(1)}, bf16[2,2,2,152,256]{4,3,2,1,0:T(8,128)(2,1)S(1)}, u32[]{:S(2)}, u32[]{:S(2)}) collective-permute-start(bf16[2,2,2,152,256]{4,3,2,1,0:T(8,128)(2,1)S(1)} %dynamic-slice_bitcast_fusion.10), channel_id=1, source_target_pairs={{0,1},{1,0},{2,3},{3,2},{4,5},{5,4},{6,7},{7,6},{8,9},{9,8},{10,11... | collective-permute-start | bytes 1867784 | tf_op jit(solution)/shard_map/ppermute | solution.py:77
  343.7 15.8 %collective-permute-start.14 = (bf16[2,2,2,32,1280]{4,3,0,1,2:T(8,128)(2,1)S(1)}, bf16[2,2,2,32,1280]{4,3,0,1,2:T(8,128)(2,1)S(1)}, u32[]{:S(2)}, u32[]{:S(2)}) collective-permute-start(bf16[2,2,2,32,1280]{4,3,0,1,2:T(8,128)(2,1)S(1)} %dynamic-slice_bitcast_fusion.9), channel_id=1, source_target_pairs={{0,4},{2,6},{4,0},{6,2},{8,12},{10,14},{12,8},{14,10},{16,20},{18,... | collective-permute-start | bytes 1966088 | tf_op jit(solution)/shard_map/ppermute | solution.py:78
  347.5 56.3 %collective-permute-start.9 = (bf16[2,2,2,64,768]{4,3,0,1,2:T(8,128)(2,1)S(1)}, bf16[2,2,2,64,768]{4,3,0,1,2:T(8,128)(2,1)S(1)}, u32[]{:S(2)}, u32[]{:S(2)}) collective-permute-start(bf16[2,2,2,64,768]{4,3,0,1,2:T(8,128)(2,1)S(1)} %dynamic-slice_bitcast_fusion.8), channel_id=1, source_target_pairs={{0,1},{1,0},{2,3},{3,2},{4,5},{5,4},{6,7},{7,6},{8,9},{9,8},{10,11... | collective-permute-start | bytes 2359304 | tf_op jit(solution)/shard_map/ppermute | solution.py:77
  359.5 12.6 %collective-permute-start.30 = (bf16[2,2,144,256]{3,2,0,1:T(8,128)(2,1)S(1)}, bf16[2,2,144,256]{3,2,0,1:T(8,128)(2,1)S(1)}, u32[]{:S(2)}, u32[]{:S(2)}) collective-permute-start(bf16[2,2,144,256]{3,2,0,1:T(8,128)(2,1)S(1)} %dynamic-slice_bitcast_fusion.20), channel_id=1, source_target_pairs={{0,1},{1,0},{2,3},{3,2},{4,5},{5,4},{6,7},{7,6},{8,9},{9,8},{10,11... | collective-permute-start | bytes 884744 | tf_op jit(solution)/shard_map/ppermute | solution.py:77
  372.2 7.2 %collective-permute-start.5 = (bf16[2,2,152,256]{3,2,1,0:T(8,128)(2,1)S(1)}, bf16[2,2,152,256]{3,2,1,0:T(8,128)(2,1)S(1)}, u32[]{:S(2)}, u32[]{:S(2)}) collective-permute-start(bf16[2,2,152,256]{3,2,1,0:T(8,128)(2,1)S(1)} %dynamic-slice_bitcast_fusion.18), channel_id=1, source_target_pairs={{0,4},{2,6},{4,0},{6,2},{8,12},{10,14},{12,8},{14,10},{16,20},{18,... | collective-permute-start | bytes 933896 | tf_op jit(solution)/shard_map/ppermute | solution.py:78
  379.4 5.9 collective-permute-start.31
  385.4 6.1 collective-permute-start.32
  391.5 7.1 %collective-permute-start.15 = (bf16[2,2,32,1280]{3,2,0,1:T(8,128)(2,1)S(1)}, bf16[2,2,32,1280]{3,2,0,1:T(8,128)(2,1)S(1)}, u32[]{:S(2)}, u32[]{:S(2)}) collective-permute-start(bf16[2,2,32,1280]{3,2,0,1:T(8,128)(2,1)S(1)} %dynamic-slice_bitcast_fusion.17), channel_id=1, source_target_pairs={{0,1},{1,0},{2,3},{3,2},{4,5},{5,4},{6,7},{7,6},{8,9},{9,8},{10,11... | collective-permute-start | bytes 983048 | tf_op jit(solution)/shard_map/ppermute | solution.py:77
  398.6 5.2 collective-permute-start.6
  403.8 108.5 %collective-permute-start.33 = (bf16[2,2,2,2,120,1280]{5,4,0,1,3,2:T(8,128)(2,1)}, bf16[2,2,2,2,120,1280]{5,4,0,1,3,2:T(8,128)(2,1)S(1)}, u32[]{:S(2)}, u32[]{:S(2)}) collective-permute-start(bf16[2,2,2,2,120,1280]{5,4,0,1,3,2:T(8,128)(2,1)} %pad_maximum_fusion), channel_id=1, source_target_pairs={{0,2},{2,0},{4,6},{6,4},{8,10},{10,8},{12,14},{14,12},{16,18},{18,... | collective-permute-start | bytes 14745608 | tf_op jit(solution)/shard_map/ppermute | solution.py:78
  403.9 7.4 %collective-permute-start.7 = (bf16[152,256]{1,0:T(8,128)(2,1)S(1)}, bf16[152,256]{1,0:T(8,128)(2,1)S(1)}, u32[]{:S(2)}, u32[]{:S(2)}) collective-permute-start(bf16[152,256]{1,0:T(8,128)(2,1)S(1)} %dynamic-slice_bitcast_fusion.30), channel_id=1, source_target_pairs={{0,16},{2,18},{4,20},{6,22},{8,24},{10,26},{12,28},{14,30},{16,0},... | collective-permute-start | bytes 233480 | tf_op jit(solution)/shard_map/ppermute | solution.py:78
  411.3 5.8 collective-permute-start.16
  417.1 9.9 %collective-permute-start.10 = (bf16[2,2,64,768]{3,2,0,1:T(8,128)(2,1)S(1)}, bf16[2,2,64,768]{3,2,0,1:T(8,128)(2,1)S(1)}, u32[]{:S(2)}, u32[]{:S(2)}) collective-permute-start(bf16[2,2,64,768]{3,2,0,1:T(8,128)(2,1)S(1)} %dynamic-slice_bitcast_fusion.16), channel_id=1, source_target_pairs={{0,4},{2,6},{4,0},{6,2},{8,12},{10,14},{12,8},{14,10},{16,20},{18,... | collective-permute-start | bytes 1179656 | tf_op jit(solution)/shard_map/ppermute | solution.py:78
  427.1 5.7 collective-permute-start.11
  432.8 10.7 %collective-permute-start.17 = (bf16[32,1280]{1,0:T(8,128)(2,1)S(1)}, bf16[32,1280]{1,0:T(8,128)(2,1)S(1)}, u32[]{:S(2)}, u32[]{:S(2)}) collective-permute-start(bf16[32,1280]{1,0:T(8,128)(2,1)S(1)} %dynamic-slice_bitcast_fusion.29), channel_id=1, source_target_pairs={{0,16},{2,18},{4,20},{6,22},{8,24},{10,26},{12,28},{14,30},{16,0},... | collective-permute-start | bytes 245768 | tf_op jit(solution)/shard_map/ppermute | solution.py:78
  436.1 10.2 %collective-permute-start.12 = (bf16[64,768]{1,0:T(8,128)(2,1)S(1)}, bf16[64,768]{1,0:T(8,128)(2,1)S(1)}, u32[]{:S(2)}, u32[]{:S(2)}) collective-permute-start(bf16[64,768]{1,0:T(8,128)(2,1)S(1)} %dynamic-slice_bitcast_fusion.28), channel_id=1, source_target_pairs={{0,16},{2,18},{4,20},{6,22},{8,24},{10,26},{12,28},{14,30},{16,0},... | collective-permute-start | bytes 294920 | tf_op jit(solution)/shard_map/ppermute | solution.py:78
  438.6 37.6 %collective-permute-start.39 = (bf16[2,2,2,128,768]{4,3,0,1,2:T(8,128)(2,1)}, bf16[2,2,2,128,768]{4,3,0,1,2:T(8,128)(2,1)}, u32[]{:S(2)}, u32[]{:S(2)}) collective-permute-start(bf16[2,2,2,128,768]{4,3,0,1,2:T(8,128)(2,1)} %dynamic-slice_bitcast_fusion.3), channel_id=1, source_target_pairs={{0,1},{1,0},{2,3},{3,2},{4,5},{5,4},{6,7},{7,6},{8,9},{9,8},{10,11... | collective-permute-start | bytes 4718600 | tf_op jit(solution)/shard_map/ppermute | solution.py:77
  440.0 39.5 %collective-permute-start.19 = (bf16[2,2,2,80,1280]{4,3,0,1,2:T(8,128)(2,1)S(1)}, bf16[2,2,2,80,1280]{4,3,0,1,2:T(8,128)(2,1)S(1)}, u32[]{:S(2)}, u32[]{:S(2)}) collective-permute-start(bf16[2,2,2,80,1280]{4,3,0,1,2:T(8,128)(2,1)S(1)} %dynamic-slice_bitcast_fusion.2), channel_id=1, source_target_pairs={{0,4},{2,6},{4,0},{6,2},{8,12},{10,14},{12,8},{14,10},{16,20},{18,... | collective-permute-start | bytes 4915208 | tf_op jit(solution)/shard_map/ppermute | solution.py:78
  443.5 67.7 %collective-permute-start.24 = (bf16[2,2,2,80,1280]{4,3,0,1,2:T(8,128)(2,1)S(1)}, bf16[2,2,2,80,1280]{4,3,0,1,2:T(8,128)(2,1)S(1)}, u32[]{:S(2)}, u32[]{:S(2)}) collective-permute-start(bf16[2,2,2,80,1280]{4,3,0,1,2:T(8,128)(2,1)S(1)} %dynamic-slice_bitcast_fusion.1), channel_id=1, source_target_pairs={{0,1},{1,0},{2,3},{3,2},{4,5},{5,4},{6,7},{7,6},{8,9},{9,8},{10,11... | collective-permute-start | bytes 4915208 | tf_op jit(solution)/shard_map/ppermute | solution.py:77
  479.0 36.3 %collective-permute-start.40 = (bf16[2,2,128,768]{3,2,0,1:T(8,128)(2,1)}, bf16[2,2,128,768]{3,2,0,1:T(8,128)(2,1)S(1)}, u32[]{:S(2)}, u32[]{:S(2)}) collective-permute-start(bf16[2,2,128,768]{3,2,0,1:T(8,128)(2,1)} %dynamic-slice_bitcast_fusion.7), channel_id=1, source_target_pairs={{0,4},{2,6},{4,0},{6,2},{8,12},{10,14},{12,8},{14,10},{16,20},{18,... | collective-permute-start | bytes 2359304 | tf_op jit(solution)/shard_map/ppermute | solution.py:78
  480.0 44.5 %collective-permute-start.20 = (bf16[2,2,80,1280]{3,2,0,1:T(8,128)(2,1)S(1)}, bf16[2,2,80,1280]{3,2,0,1:T(8,128)(2,1)S(1)}, u32[]{:S(2)}, u32[]{:S(2)}) collective-permute-start(bf16[2,2,80,1280]{3,2,0,1:T(8,128)(2,1)S(1)} %dynamic-slice_bitcast_fusion.6), channel_id=1, source_target_pairs={{0,1},{1,0},{2,3},{3,2},{4,5},{5,4},{6,7},{7,6},{8,9},{9,8},{10,11... | collective-permute-start | bytes 2457608 | tf_op jit(solution)/shard_map/ppermute | solution.py:77
  511.7 21.2 %collective-permute-start.25 = (bf16[2,2,80,1280]{3,2,0,1:T(8,128)(2,1)S(1)}, bf16[2,2,80,1280]{3,2,0,1:T(8,128)(2,1)S(1)}, u32[]{:S(2)}, u32[]{:S(2)}) collective-permute-start(bf16[2,2,80,1280]{3,2,0,1:T(8,128)(2,1)S(1)} %dynamic-slice_bitcast_fusion.5), channel_id=1, source_target_pairs={{0,4},{2,6},{4,0},{6,2},{8,12},{10,14},{12,8},{14,10},{16,20},{18,... | collective-permute-start | bytes 2457608 | tf_op jit(solution)/shard_map/ppermute | solution.py:78
  513.7 62.3 %collective-permute-start.34 = (bf16[2,2,2,120,1280]{4,3,0,1,2:T(8,128)(2,1)S(1)}, bf16[2,2,2,120,1280]{4,3,0,1,2:T(8,128)(2,1)S(1)}, u32[]{:S(2)}, u32[]{:S(2)}) collective-permute-start(bf16[2,2,2,120,1280]{4,3,0,1,2:T(8,128)(2,1)S(1)} %dynamic-slice_bitcast_fusion), channel_id=1, source_target_pairs={{0,4},{2,6},{4,0},{6,2},{8,12},{10,14},{12,8},{14,10},{16,20},{18,... | collective-permute-start | bytes 7372808 | tf_op jit(solution)/shard_map/ppermute | solution.py:78
  515.5 17.6 %collective-permute-start.41 = (bf16[2,128,768]{2,1,0:T(8,128)(2,1)S(1)}, bf16[2,128,768]{2,1,0:T(8,128)(2,1)S(1)}, u32[]{:S(2)}, u32[]{:S(2)}) collective-permute-start(bf16[2,128,768]{2,1,0:T(8,128)(2,1)S(1)} %dynamic-slice_bitcast_fusion.15), channel_id=1, source_target_pairs={{0,8},{2,10},{4,12},{6,14},{8,0},{10,2},{12,4},{14,6},{16,24},{18,... | collective-permute-start | bytes 1179656 | tf_op jit(solution)/shard_map/ppermute | solution.py:78
  524.7 18.0 %collective-permute-start.21 = (bf16[2,80,1280]{2,1,0:T(8,128)(2,1)S(1)}, bf16[2,80,1280]{2,1,0:T(8,128)(2,1)S(1)}, u32[]{:S(2)}, u32[]{:S(2)}) collective-permute-start(bf16[2,80,1280]{2,1,0:T(8,128)(2,1)S(1)} %dynamic-slice_bitcast_fusion.14), channel_id=1, source_target_pairs={{0,8},{2,10},{4,12},{6,14},{8,0},{10,2},{12,4},{14,6},{16,24},{18,... | collective-permute-start | bytes 1228808 | tf_op jit(solution)/shard_map/ppermute | solution.py:78
  533.3 7.4 %collective-permute-start.42 = (bf16[128,768]{1,0:T(8,128)(2,1)S(1)}, bf16[128,768]{1,0:T(8,128)(2,1)S(1)}, u32[]{:S(2)}, u32[]{:S(2)}) collective-permute-start(bf16[128,768]{1,0:T(8,128)(2,1)S(1)} %dynamic-slice_bitcast_fusion.23), channel_id=1, source_target_pairs={{0,16},{2,18},{4,20},{6,22},{8,24},{10,26},{12,28},{14,30},{16,0},... | collective-permute-start | bytes 589832 | tf_op jit(solution)/shard_map/ppermute | solution.py:78
  536.3 43.4 %collective-permute-start.26 = (bf16[2,80,1280]{2,1,0:T(8,128)(2,1)S(1)}, bf16[2,80,1280]{2,1,0:T(8,128)(2,1)S(1)}, u32[]{:S(2)}, u32[]{:S(2)}) collective-permute-start(bf16[2,80,1280]{2,1,0:T(8,128)(2,1)S(1)} %dynamic-slice_bitcast_fusion.13), channel_id=1, source_target_pairs={{0,8},{2,10},{4,12},{6,14},{8,0},{10,2},{12,4},{14,6},{16,24},{18,... | collective-permute-start | bytes 1228808 | tf_op jit(solution)/shard_map/ppermute | solution.py:78
  576.8 19.5 %collective-permute-start.35 = (bf16[2,2,120,1280]{3,2,0,1:T(8,128)(2,1)S(1)}, bf16[2,2,120,1280]{3,2,0,1:T(8,128)(2,1)S(1)}, u32[]{:S(2)}, u32[]{:S(2)}) collective-permute-start(bf16[2,2,120,1280]{3,2,0,1:T(8,128)(2,1)S(1)} %dynamic-slice_bitcast_fusion.4), channel_id=1, source_target_pairs={{0,1},{1,0},{2,3},{3,2},{4,5},{5,4},{6,7},{7,6},{8,9},{9,8},{10,11... | collective-permute-start | bytes 3686408 | tf_op jit(solution)/shard_map/ppermute | solution.py:77
  577.3 11.1 %collective-permute-start.22 = (bf16[80,1280]{1,0:T(8,128)(2,1)S(1)}, bf16[80,1280]{1,0:T(8,128)(2,1)S(1)}, u32[]{:S(2)}, u32[]{:S(2)}) collective-permute-start(bf16[80,1280]{1,0:T(8,128)(2,1)S(1)} %dynamic-slice_bitcast_fusion.22), channel_id=1, source_target_pairs={{0,16},{2,18},{4,20},{6,22},{8,24},{10,26},{12,28},{14,30},{16,0},... | collective-permute-start | bytes 614408 | tf_op jit(solution)/shard_map/ppermute | solution.py:78
  579.9 19.2 %collective-permute-start.27 = (bf16[80,1280]{1,0:T(8,128)(2,1)S(1)}, bf16[80,1280]{1,0:T(8,128)(2,1)S(1)}, u32[]{:S(2)}, u32[]{:S(2)}) collective-permute-start(bf16[80,1280]{1,0:T(8,128)(2,1)S(1)} %dynamic-slice_bitcast_fusion.21), channel_id=1, source_target_pairs={{0,16},{2,18},{4,20},{6,22},{8,24},{10,26},{12,28},{14,30},{16,0},... | collective-permute-start | bytes 614408 | tf_op jit(solution)/shard_map/ppermute | solution.py:78
  596.6 13.5 %collective-permute-start.36 = (bf16[2,120,1280]{2,1,0:T(8,128)(2,1)S(1)}, bf16[2,120,1280]{2,1,0:T(8,128)(2,1)S(1)}, u32[]{:S(2)}, u32[]{:S(2)}) collective-permute-start(bf16[2,120,1280]{2,1,0:T(8,128)(2,1)S(1)} %dynamic-slice_bitcast_fusion.11), channel_id=1, source_target_pairs={{0,8},{2,10},{4,12},{6,14},{8,0},{10,2},{12,4},{14,6},{16,24},{18,... | collective-permute-start | bytes 1843208 | tf_op jit(solution)/shard_map/ppermute | solution.py:78
  610.3 12.1 %copy-start.1 = (bf16[1280,1280]{1,0:T(8,128)(2,1)S(1)}, bf16[1280,1280]{1,0:T(8,128)(2,1)}, u32[]{:S(2)}) copy-start(bf16[1280,1280]{1,0:T(8,128)(2,1)} %param.55) | copy-start | bytes 9830404
  610.4 11.1 %collective-permute-start.37 = (bf16[120,1280]{1,0:T(8,128)(2,1)S(1)}, bf16[120,1280]{1,0:T(8,128)(2,1)S(1)}, u32[]{:S(2)}, u32[]{:S(2)}) collective-permute-start(bf16[120,1280]{1,0:T(8,128)(2,1)S(1)} %dynamic-slice_bitcast_fusion.19), channel_id=1, source_target_pairs={{0,16},{2,18},{4,20},{6,22},{8,24},{10,26},{12,28},{14,30},{16,0},... | collective-permute-start | bytes 921608 | tf_op jit(solution)/shard_map/ppermute | solution.py:78
  (198 other events, 465.5 us)
where the time goes:
time: 629 us; the launch traced here: 623 us
  waiting for transfers between devices  228 us (36%)
  matrix products  157 us (25%)
  local copies, waits for them, and re-layouts  124 us (20%)
  other arithmetic  55.2 us (9%)
  starting transfers between devices  41.4 us (7%)
  Pallas kernels  12.9 us (2%)
    ppermute x32, waiting for transfers between devices, exchange(): lax.ppermute(x, 'items', [(i, i ^ 1 << name) for i in range(self.n_items)])  133 us
    ppermute x8, waiting for transfers between devices, exchange(): return lax.ppermute(x, 'blk', [(0, 1), (1, 0)])  95 us
    unnamed x445, local copies, waits for them, and re-layouts  59.7 us
    dot_general x22, matrix products, tn(): lax.dot_general(a, b, (((0,), (0,)), ((), ())), preferred_element_type=F32)  51.7 us
    dot_general x20, matrix products, nn(): lax.dot_general(a, b, (((1,), (0,)), ((), ())), preferred_element_type=F32)  45.2 us
    dot_general x21, matrix products, nt(): lax.dot_general(a, b, (((1,), (1,)), ((), ())), preferred_element_type=F32)  40.2 us
    ppermute x32, starting transfers between devices, exchange(): lax.ppermute(x, 'items', [(i, i ^ 1 << name) for i in range(self.n_items)])  31.2 us
    convert_element_type x32, other arithmetic, reduce(): parts = [total if last else total.astype(BF16)]  18.4 us
  transfers between devices with their start and end apart: 43, of which 23 were waited for; matrix products, arithmetic and copies ran while one was open for 26% of the time, Pallas kernels for 2%

commit v1 on v0

--- a/solution.py
+++ b/solution.py
@@ -1,6 +1,8 @@
 import jax
 import jax.numpy as jnp
 from jax import lax
+from jax.experimental import pallas as pl
+from jax.experimental.pallas import tpu as pltpu
 from jax.sharding import PartitionSpec as P
 
 HEADS = 8
@@ -105,6 +107,322 @@
         return out
 
 
+CHUNK = 256
+LAG = 2
+MESH = pl.DeviceIdType.MESH
+STAGES = {"xy": ("c", "x", "y", "z0", "z1"), "yx": ("c", "y", "x", "z0", "z1")}
+ITEM_BIT = {"c": 0, "x": 1, "z0": 2, "z1": 3}
+
+
+def padded_rows(r):
+    return -(-r // 16) * 16
+
+
+def my_bit(name):
+    if name == "y":
+        return lax.axis_index("blk")
+    return (lax.axis_index("items") // 2 ** ITEM_BIT[name]) % 2
+
+
+def partner(name):
+    if name == "y":
+        return {"blk": 1 - lax.axis_index("blk")}
+    return {"items": lax.axis_index("items") + (1 - 2 * my_bit(name)) * 2 ** ITEM_BIT[name]}
+
+
+def divide(first, second, mine, r, by_rows):
+    if by_rows:
+        first, second = (
+            jnp.concatenate([first[:r], second[:r]], axis=0),
+            jnp.concatenate([first[r:], second[r:]], axis=0),
+        )
+    return jnp.where(mine == 0, first, second), jnp.where(mine == 0, second, first)
+
+
+class Chunk:
+    def __init__(self, bufs, at, sems, r, width, order):
+        self.rc, self.r1, self.r2, self.r3, self.s4, self.r4, self.out = [b.at[at] for b in bufs]
+        self.send, self.recv, self.at = sems[0], sems[1], at
+        self.r, self.width, self.order = r, width, order
+        self.step = 256 if r <= 40 and width % 256 == 0 else 128
+
+    def copy(self, stage, source=None):
+        src, dst = (
+            (source, self.rc),
+            (self.rc.at[:, :, 1], self.r1),
+            (self.rc.at[:, 1, 0], self.r2),
+            (self.rc.at[1, 0, 0], self.r3),
+            (self.s4, self.r4),
+        )[stage]
+        return pltpu.make_async_remote_copy(
+            src_ref=dst if src is None else src,
+            dst_ref=dst,
+            send_sem=self.send.at[self.at, stage],
+            recv_sem=self.recv.at[self.at, stage],
+            device_id=partner(STAGES[self.order][stage]),
+            device_id_type=MESH,
+        )
+
+    def loop(self, pairs, body):
+        columns = self.width // self.step
+
+        def run(i, carry):
+            body(i // columns, pl.ds(pl.multiple_of((i % columns) * self.step, self.step), self.step))
+            return carry
+
+        lax.fori_loop(0, pairs * columns, run, 0)
+
+    def advance(self, stage, loaded=None):
+        self.copy(stage).wait_recv()
+        names = STAGES[self.order]
+        r, kind, rc = self.r, self.rc.dtype, self.rc
+        mine = my_bit(names[stage + 1]) if stage < 4 else None
+
+        def total(a, b):
+            return a.astype(F32) + b.astype(F32)
+
+        def stage0(p, cols):
+            q, z = p // 2, p % 2
+            first = total(rc[q, z, 0, :, cols], loaded[q, z, 0, :, cols])
+            second = total(rc[q, z, 1, :, cols], loaded[q, z, 1, :, cols])
+            keep, send = divide(first, second, mine, r, self.order == "yx")
+            rc[q, z, 0, :, cols] = keep.astype(kind)
+            rc[q, z, 1, :, cols] = send.astype(kind)
+
+        def stage1(q, cols):
+            first = total(rc[q, 0, 0, :, cols], self.r1[q, 0, :, cols])
+            second = total(rc[q, 1, 0, :, cols], self.r1[q, 1, :, cols])
+            keep, send = divide(first, second, mine, r, True)
+            rc[q, 0, 0, :, cols] = keep.astype(kind)
+            rc[q, 1, 0, :, cols] = send.astype(kind)
+
+        def stage2(q, cols):
+            first = total(rc[0, 0, 0, :, cols], self.r2[0, :, cols])
+            second = total(rc[1, 0, 0, :, cols], self.r2[1, :, cols])
+            keep, send = divide(first, second, mine, r, True)
+            rc[0, 0, 0, :, cols] = keep.astype(kind)
+            rc[1, 0, 0, :, cols] = send.astype(kind)
+
+        def stage3(q, cols):
+            both = total(rc[0, 0, 0, :, cols], self.r3[:, cols])
+            keep = jnp.where(mine == 0, both[:r], both[r:])
+            send = jnp.where(mine == 0, both[r:], both[:r])
+            extra = padded_rows(r) - r
+            if extra:
+                send = jnp.concatenate([send, jnp.zeros((extra, send.shape[1]), F32)], axis=0)
+            self.s4[:, cols] = send.astype(kind)
+            self.out[:, cols] = keep
+
+        def stage4(q, cols):
+            self.out[:, cols] = self.out[:, cols] + self.r4[:, cols].astype(F32)[:r]
+
+        self.loop((4, 2, 1, 1, 1)[stage], (stage0, stage1, stage2, stage3, stage4)[stage])
+        if stage < 4:
+            self.copy(stage + 1).start()
+
+
+def when(condition, action):
+    if isinstance(condition, bool):
+        if condition:
+            action()
+    else:
+        pl.when(condition)(action)
+
+
+def reduce_kernel(plan, *refs):
+    widths, segments, others, steps = plan
+    n_a, n_o = len(widths), len(others)
+    a_src, o_src = refs[:n_a], refs[n_a : n_a + n_o]
+    refs = refs[n_a + n_o :]
+    a_out, o_out = refs[:n_a], refs[n_a : n_a + n_o]
+    refs = refs[n_a + n_o :]
+    a_bufs, refs = refs[:7], refs[7:]
+    loads, refs = refs[0], refs[1:]
+    o_bufs, refs = [refs[8 * i : 8 * i + 8] for i in range(n_o)], refs[8 * n_o :]
+    a_sems, o_sems, load_sem, o_load_sem, a_out_sem, o_out_sem = refs[0:2], refs[2:4], refs[4], refs[5], refs[6], refs[7]
+    core = my_bit("c")
+
+    barrier = pltpu.get_barrier_semaphore()
+    for name in ("c", "x", "y", "z0", "z1"):
+        pl.semaphore_signal(barrier, inc=1, device_id=partner(name), device_id_type=MESH)
+    pl.semaphore_wait(barrier, 5)
+
+    def chunk(step, side):
+        return Chunk(a_bufs, 2 * step + side, a_sems, 40, CHUNK, ("xy", "yx")[side])
+
+    def columns(number):
+        start = number * CHUNK
+        return pl.ds(start if isinstance(number, int) else pl.multiple_of(start, CHUNK), CHUNK)
+
+    def first_copy(segment, j, side):
+        array, start = segments[segment][side]
+        base = sum(seg[2] for seg in segments[:segment])
+        return chunk(base + j, side).copy(0, a_src[array].at[:, :, :, 1 - core, :, columns(start + j)])
+
+    def load(segment, step, j, side):
+        array, start = segments[segment][side]
+        slot = 2 * (step % 2) + side
+        return pltpu.make_async_copy(
+            a_src[array].at[:, :, :, core, :, columns(start + j)], loads.at[slot], load_sem.at[slot]
+        )
+
+    small = []
+    for i, (r, width, order) in enumerate(others):
+        rc, load_buf = o_bufs[i][0], o_bufs[i][7]
+        item = Chunk([b.at[0:1] for b in o_bufs[i][:7]], 0, o_sems, r, width, order)
+        item.at = i
+        small.append(item)
+        item.copy(0, o_src[i].at[:, :, :, 1 - core]).start()
+        pltpu.make_async_copy(o_src[i].at[:, :, :, core], load_buf, o_load_sem.at[i]).start()
+    for j in range(segments[0][2]):
+        for side in range(2):
+            first_copy(0, j, side).start()
+    for i, item in enumerate(small):
+        pltpu.make_async_copy(o_src[i].at[:, :, :, core], o_bufs[i][7], o_load_sem.at[i]).wait()
+        item.advance(0, o_bufs[i][7])
+
+    def lagged(step):
+        for stage in range(4, 0, -1):
+            old = step - stage * LAG
+            if isinstance(step, int):
+                go = 0 <= old < steps
+            else:
+                go = jnp.logical_and(old >= 0, old < steps)
+
+            def act(old=old, stage=stage):
+                for side in range(2):
+                    chunk(old, side).advance(stage)
+
+            when(go, act)
+
+    base = 0
+    for number, segment in enumerate(segments):
+        count = segment[2]
+        if number + 1 < len(segments):
+            for j in range(segments[number + 1][2]):
+                for side in range(2):
+                    first_copy(number + 1, j, side).start()
+        for side in range(2):
+            load(number, base, 0, side).start()
+
+        def step_body(j, number=number, base=base, count=count):
+            step = base + j
+
+            def ahead():
+                for side in range(2):
+                    load(number, step + 1, j + 1, side).start()
+
+            when(j + 1 < count, ahead)
+            for side in range(2):
+                load(number, step, j, side).wait()
+                chunk(step, side).advance(0, loads.at[2 * (step % 2) + side])
+            lagged(step)
+
+        if count > 1:
+
+            def run(j, carry):
+                step_body(j)
+                return carry
+
+            lax.fori_loop(0, count, run, 0)
+        else:
+            step_body(0)
+        base += count
+        if number < 4:
+            for item in small:
+                item.advance(number + 1)
+
+    def drain(step, carry):
+        lagged(step)
+        return carry
+
+    lax.fori_loop(steps, steps + 4 * LAG, drain, 0)
+
+    outs = []
+    for number, segment in enumerate(segments):
+        base = sum(seg[2] for seg in segments[:number])
+        for side in range(2):
+            array, start = segment[side]
+            for j in range(segment[2]):
+                at = 2 * (base + j) + side
+                outs.append(
+                    pltpu.make_async_copy(
+                        a_bufs[6].at[at], a_out[array].at[:, columns(start + j)], a_out_sem.at[at]
+                    )
+                )
+    for i in range(n_o):
+        outs.append(pltpu.make_async_copy(o_bufs[i][6].at[0], o_out[i], o_out_sem.at[i]))
+    for copy in outs:
+        copy.start()
+    for number, segment in enumerate(segments):
+        for j in range(segment[2]):
+            for side in range(2):
+                first_copy(number, j, side).wait_send()
+    for i, item in enumerate(small):
+        item.copy(0, o_src[i].at[:, :, :, 1 - core]).wait_send()
+        for stage in range(1, 5):
+            item.copy(stage).wait_send()
+
+    def wait_sent(step, carry):
+        for side in range(2):
+            for stage in range(1, 5):
+                chunk(step, side).copy(stage).wait_send()
+        return carry
+
+    lax.fori_loop(0, steps, wait_sent, 0)
+    for copy in outs:
+        copy.wait()
+
+
+def buffers(count, r, width, kind):
+    rp = padded_rows(r)
+    return [
+        pltpu.VMEM((count, 2, 2, 2, 2 * r, width), kind),
+        pltpu.VMEM((count, 2, 2, 2 * r, width), kind),
+        pltpu.VMEM((count, 2, 2 * r, width), kind),
+        pltpu.VMEM((count, 2 * r, width), kind),
+        pltpu.VMEM((count, rp, width), kind),
+        pltpu.VMEM((count, rp, width), kind),
+        pltpu.VMEM((count, r, width), F32),
+    ]
+
+
+def reduce_all(tall, segments, others):
+    steps = sum(segment[2] for segment in segments)
+
+    def view(g):
+        return g.reshape(2, 2, 2, 2, g.shape[0] // 16, g.shape[1])
+
+    plan = (
+        tuple(g.shape[1] for g in tall),
+        segments,
+        tuple((g.shape[0] // 32, g.shape[1], order) for g, order in others),
+        steps,
+    )
+    scratch = buffers(2 * steps, 40, CHUNK, BF16)
+    scratch.append(pltpu.VMEM((4, 2, 2, 2, 80, CHUNK), BF16))
+    for g, order in others:
+        r = g.shape[0] // 32
+        scratch += buffers(1, r, g.shape[1], g.dtype)
+        scratch.append(pltpu.VMEM((2, 2, 2, 2 * r, g.shape[1]), g.dtype))
+    dma = pltpu.SemaphoreType.DMA
+    scratch += [dma((2 * steps, 5)), dma((2 * steps, 5)), dma((len(others), 5)), dma((len(others), 5))]
+    scratch += [dma((4,)), dma((len(others),)), dma((2 * steps,)), dma((len(others),))]
+    arrays = list(tall) + [g for g, order in others]
+    anywhere = pl.BlockSpec(memory_space=pl.ANY)
+    results = pl.pallas_call(
+        lambda *refs: reduce_kernel(plan, *refs),
+        out_shape=[jax.ShapeDtypeStruct((g.shape[0] // 32, g.shape[1]), F32) for g in arrays],
+        in_specs=[anywhere] * len(arrays),
+        out_specs=[anywhere] * len(arrays),
+        scratch_shapes=scratch,
+        compiler_params=pltpu.CompilerParams(
+            collective_id=0, has_side_effects=True, vmem_limit_bytes=60 * 1024 * 1024
+        ),
+    )(*[view(g) for g in arrays])
+    return results[: len(tall)], results[len(tall) :]
+
+
 def local(
     byte_ids, span_start, span_len, embedding, position, mask_vector, gain_bytes, key_enc,
     value_enc, latent_init, gain_latent, query_enc, out_enc, gain_enc_mlp, up_enc, down_enc,
@@ -140,7 +458,7 @@
     places = lax.iota(jnp.int32, total)
     inside = (places[None, :] >= starts[:, None]) & (places[None, :] < (starts + lengths)[:, None])
     codes = jnp.where(jnp.any(inside, axis=0), vocab, ids)
-    padded = 512
+    padded = -(-(vocab + 1) // 128) * 128
     table = jnp.concatenate(
         [embedding, mask_vector[None, :], jnp.zeros((padded - vocab - 1, embedding.shape[1]), BF16)], axis=0
     )
@@ -205,7 +523,7 @@
     logits_out = jnp.stack([jnp.where(me == 0, mine, got), jnp.where(me == 0, got, mine)])
 
     dnf = nn(cot, embedding)
-    g_emb_out = tn(nf, cot)
+    g_emb_out = tn(nf, jnp.pad(cot, ((0, 0), (0, padded - vocab))))
     ddec, g_gain_final = norm_backward(dnf, hat_f, rstd_f, gain_final)
     ddec16 = ddec.astype(BF16)
     da_d = nt(ddec16, out_dec)
@@ -272,67 +590,69 @@
     g_value_enc = tn(nb, dv_e)
     dnb = nt(dk_e, key_enc) + nt(dv_e, value_enc)
     dbytes, g_gain_bytes = norm_backward(dnb, hat_b, rstd_b, gain_bytes)
-    g_table = tn(dbytes.astype(BF16), onehot)
-    g_emb = jnp.concatenate(
-        [
-            g_table[:, :vocab] + g_emb_out,
-            g_table[:, vocab : vocab + 1],
-            g_gain_bytes[:, None],
-            g_gain_dec_q[:, None],
-            g_gain_final[:, None],
-            jnp.zeros((g_table.shape[0], padded - vocab - 4), F32),
-        ],
-        axis=1,
-    )
-    g_gains = jnp.stack(
-        [g_gain_latent, g_gain_enc_mlp, g_gain_self, g_gain_self_mlp, g_gain_dec_kv], axis=1
-    )
-    g_gains = jnp.pad(g_gains, ((0, 0), (0, 256 - 5)))
-
-    r_dec_query, r_out_dec, r_value_dec = reducer.reduce([g_dec_query, g_out_dec, g_value_dec], order_yx)
-    r_down_self, r_up_self, r_out_self = reducer.reduce([g_down_self, g_up_self, g_out_self], order_xy)
-    r_value_self, r_down_enc = reducer.reduce([g_value_self, g_down_enc], order_yx)
-    r_up_enc, r_out_enc = reducer.reduce([g_up_enc, g_out_enc], order_xy)
-    r_query_dec, r_key_dec, r_query_self, r_key_self = reducer.reduce(
-        [g_query_dec, g_key_dec, g_query_self, g_key_self], order_xy
-    )
-    r_value_enc, r_latent = reducer.reduce([g_value_enc, g_latent], order_xy)
-    (r_position,) = reducer.reduce([dbytes], order_yx)
-    r_key_enc, r_query_enc, r_gains, r_emb_a, r_emb_b = reducer.reduce(
-        [g_key_enc, g_query_enc, g_gains, g_emb[:, :256], g_emb[:, 256:]], order_yx
-    )
-    r_emb = jnp.concatenate([r_emb_a, r_emb_b], axis=1)
+    g_table = tn(dbytes.astype(BF16), onehot) + g_emb_out
+    wide_gains = [g_gain_latent, g_gain_enc_mlp, g_gain_self, g_gain_self_mlp, g_gain_dec_kv]
+    byte_gains = [g_gain_bytes, g_gain_dec_q, g_gain_final]
+    count = reducer.count
+    vectors = jnp.concatenate([g.reshape(count, -1) for g in wide_gains + byte_gains], axis=1)
+    length = vectors.shape[1]
+    vectors = jnp.pad(vectors, ((0, 0), (0, 1024 - length))).reshape(count * 8, 128)
+
+    if reducer.n_items == 16:
+        low = lambda g: g.astype(BF16)
+        tall = [
+            g_up_enc, g_down_enc, g_out_enc, g_down_self, g_up_self, g_out_self,
+            g_value_self, g_value_dec, g_key_self, g_query_self, g_key_dec, g_query_enc,
+        ]
+        segments = (
+            ((0, 0), (1, 0), 5),
+            ((2, 0), (3, 0), 5),
+            ((4, 0), (5, 0), 5),
+            ((6, 0), (7, 0), 3),
+            ((6, 3), (8, 0), 1),
+            ((6, 4), (9, 0), 1),
+            ((10, 0), (11, 0), 1),
+        )
+        others = [
+            (low(g_dec_query), "xy"), (low(dbytes), "yx"), (low(g_value_enc), "xy"), (low(g_out_dec), "yx"),
+            (low(g_table), "yx"), (low(g_key_enc), "xy"), (low(g_query_dec), "yx"), (low(g_latent), "xy"),
+            (vectors, "yx"),
+        ]
+        (
+            r_up_enc, r_down_enc, r_out_enc, r_down_self, r_up_self, r_out_self,
+            r_value_self, r_value_dec, r_key_self, r_query_self, r_key_dec, r_query_enc,
+        ), (
+            r_dec_query, r_position, r_value_enc, r_out_dec, r_emb, r_key_enc, r_query_dec, r_latent, r_vectors,
+        ) = reduce_all([low(g) for g in tall], segments, others)
+    else:
+        r_dec_query, r_out_dec, r_value_dec = reducer.reduce([g_dec_query, g_out_dec, g_value_dec], order_yx)
+        r_down_self, r_up_self, r_out_self = reducer.reduce([g_down_self, g_up_self, g_out_self], order_xy)
+        r_value_self, r_down_enc = reducer.reduce([g_value_self, g_down_enc], order_yx)
+        r_up_enc, r_out_enc = reducer.reduce([g_up_enc, g_out_enc], order_xy)
+        r_query_dec, r_key_dec, r_query_self, r_key_self = reducer.reduce(
+            [g_query_dec, g_key_dec, g_query_self, g_key_self], order_xy
+        )
+        r_value_enc, r_latent = reducer.reduce([g_value_enc, g_latent], order_xy)
+        (r_position,) = reducer.reduce([dbytes], order_yx)
+        r_key_enc, r_query_enc = reducer.reduce([g_key_enc, g_query_enc], order_yx)
+        (r_emb,) = reducer.reduce([g_table], order_yx)
+        (r_vectors,) = reducer.reduce([vectors], order_xy)
+
+    flat = r_vectors.reshape(-1)
+    pieces, at = [], 0
+    for g in wide_gains + byte_gains:
+        size = g.shape[0] // count
+        pieces.append(flat[at : at + size])
+        at += size
+    (
+        r_gain_latent, r_gain_enc_mlp, r_gain_self, r_gain_self_mlp, r_gain_dec_kv,
+        r_gain_bytes, r_gain_dec_q, r_gain_final,
+    ) = pieces
     return (
-        logits_out,
-        r_emb[:, :vocab].T,
-        r_position,
-        r_emb[:, vocab],
-        r_emb[:, vocab + 1],
-        r_key_enc,
-        r_value_enc,
-        r_latent,
-        r_gains[:, 0],
-        r_query_enc,
-        r_out_enc,
-        r_gains[:, 1],
-        r_up_enc,
-        r_down_enc,
-        r_gains[:, 2],
-        r_query_self,
-        r_key_self,
-        r_value_self,
-        r_out_self,
-        r_gains[:, 3],
-        r_up_self,
-        r_down_self,
-        r_gains[:, 4],
-        r_key_dec,
-        r_value_dec,
-        r_dec_query,
-        r_emb[:, vocab + 2],
-        r_query_dec,
-        r_out_dec,
-        r_emb[:, vocab + 3],
+        logits_out, r_emb[:, :vocab].T, r_position, r_emb[:, vocab], r_gain_bytes, r_key_enc, r_value_enc,
+        r_latent, r_gain_latent, r_query_enc, r_out_enc, r_gain_enc_mlp, r_up_enc, r_down_enc, r_gain_self,
+        r_query_self, r_key_self, r_value_self, r_out_self, r_gain_self_mlp, r_up_self, r_down_self,
+        r_gain_dec_kv, r_key_dec, r_value_dec, r_dec_query, r_gain_dec_q, r_query_dec, r_out_dec, r_gain_final,
     )
 
 

time: 629 us -> 465 us (0.74)
  waiting for transfers between devices: 228 us -> 0.01 us
  Pallas kernels: 12.9 us -> 201 us
  local copies, waits for them, and re-layouts: 124 us -> 52.4 us
  starting transfers between devices: 41.4 us -> 5.06 us
  other arithmetic: 55.2 us -> 34.2 us
  matrix products: 157 us -> 164 us
    ppermute x40 -> x0, waiting for transfers between devices: 228 us -> none  [the longest x32 133 us: exchange(): lax.ppermute(x, 'items', [(i, i ^ 1 << name) for i in range(self.n_items)])]
    pallas_call x0 -> x1, Pallas kernels: none -> 188 us  [reduce_all(): pl.pallas_call(lambda *refs: reduce_kernel(plan, *refs), out_shape=[jax.S...]
    ppermute x40 -> x0, starting transfers between devices: 36.4 us -> none  [the longest x32 31.2 us: exchange(): lax.ppermute(x, 'items', [(i, i ^ 1 << name) for i in range(self.n_items)])]
    dynamic_slice x50 -> x0, local copies, waits for them, and re-layouts: 23.2 us -> none  [the longest x33 15.1 us: reduce(): lax.dynamic_index_in_dim(p, mine, axis, keepdims=False)]
    unnamed x445 -> x375, local copies, waits for them, and re-layouts: 59.7 us -> 37.1 us
    convert_element_type x35 -> x3, other arithmetic: 25.7 us -> 10.7 us  [local(): low = lambda g: g.astype(BF16)]
    slice x19 -> x3, local copies, waits for them, and re-layouts: 17 us -> 4.23 us  [the longest x2 2.83 us: local(): pieces.append(flat[at:at + size])]
    concatenate x2 -> x1, local copies, waits for them, and re-layouts: 9.18 us -> 0.1 us  [local(): jnp.concatenate([g.reshape(count, -1) for g in wide_gains + byte_gains],...]
  transfers between devices with their start and end apart: 43 -> 3, of which waited for: 23 -> 0; matrix products, arithmetic and copies ran while one was open for 26% -> 22% of each run, Pallas kernels for 2% -> 44%
where the time goes in v1:
time: 465 us; the launch traced here: 459 us
  Pallas kernels  201 us (43%)
  matrix products  164 us (35%)
  local copies, waits for them, and re-layouts  52.4 us (11%)
  other arithmetic  34.2 us (7%)
  starting transfers between devices  5.06 us (1%)
    pallas_call x1, Pallas kernels, reduce_all(): pl.pallas_call(lambda *refs: reduce_kernel(plan, *refs), out_shape=[jax.S...  188 us
    dot_general x22, matrix products, tn(): lax.dot_general(a, b, (((0,), (0,)), ((), ())), preferred_element_type=F32)  54.8 us
    dot_general x21, matrix products, nt(): lax.dot_general(a, b, (((1,), (1,)), ((), ())), preferred_element_type=F32)  44.8 us
    dot_general x20, matrix products, nn(): lax.dot_general(a, b, (((1,), (0,)), ((), ())), preferred_element_type=F32)  44.6 us
    unnamed x375, local copies, waits for them, and re-layouts  37.1 us
    dot_general x5, matrix products, bdot(): lax.dot_general(a, b, (((ca,), (cb,)), ((0,), (0,))), preferred_element_t...  16.1 us
    unnamed x2, Pallas kernels  12.8 us
    convert_element_type x3, other arithmetic, local(): low = lambda g: g.astype(BF16)  10.7 us
  transfers between devices with their start and end apart: 3, of which 0 were waited for; matrix products, arithmetic and copies ran while one was open for 22% of the time, Pallas kernels for 44%

profile of v1, /device:TPU:0, one launch (start us, length us, event | category | flops | bytes accessed | tf_op | source)
XLA Modules:
  0.0 459.4 jit_solution(16703511863108837661)
XLA Ops:
  1.6 3.0 collective-permute-start
  4.6 4.9 %constant_dynamic-slice_fusion.1 = (bf16[1,1024,262]{1,0,2:T(2,128)(2,1)}, bf16[1,1024,262]{1,0,2:T(2,128)(2,1)S(1)}) fusion(bf16[2,1024,262]{1,0,2:T(2,128)(2,1)} %param.65, s32[]{:T(128)S(6)} %select_n.62, s32[]{:T(128)S(6)} %select_n.64), kind=kLoop, calls=%fused_computation.238 | loop fusion | bytes 2146312 | tf_op jit(solution)/shard_map/jit(dynamic_index_in_dim)/dynamic_slice | solution.py:447
  14.3 2.0 convolution_convert_fusion.22
  18.3 4.3 fusion.138
  23.5 1.7 copy-done.2
  29.0 6.8 %fusion.147 = f32[2048,1280]{1,0:T(8,128)} fusion(bf16[2048,768]{1,0:T(8,128)(2,1)S(1)} %multiply_convert_fusion.2, bf16[768,1280]{1,0:T(8,128)(2,1)S(1)} %copy-done.155), kind=kOutput, calls=%fused_computation.287 | convolution fusion | flops 4026531840 | bytes 15597568 | tf_op jit(solution)/shard_map/dot_general | solution.py:17
  38.7 7.3 %online-softmax = f32[256,1280]{1,0:T(8,128)} custom-call(f32[256,2048]{1,0:T(8,128)} %copy-done.3, f32[2048,1280]{1,0:T(8,128)} %fusion.147), custom_call_target="tpu_custom_call" | custom-call | tf_op online-softmax
  46.0 3.7 fusion.139
  56.6 1.9 convolution_convert_fusion.20
  58.5 2.2 copy.85
  60.7 3.7 fusion.141
  64.3 3.2 convolution_convert_fusion.23
  67.5 3.6 fusion.142
  77.9 1.6 fusion.148
  81.4 1.4 fusion.29
  82.8 5.5 %online-softmax.1 = f32[2048,768]{1,0:T(8,128)} custom-call(f32[2048,256]{1,0:T(8,128)} %copy-done.7, f32[256,768]{1,0:T(8,128)} %fusion.148), custom_call_target="tpu_custom_call" | custom-call | tf_op online-softmax
  88.3 6.9 %fusion.144 = (f32[2048]{0:T(1024)S(1)}, f32[2048,768]{1,0:T(8,128)S(1)}) fusion(bf16[768,768]{1,0:T(8,128)(2,1)} %param.63, f32[2048,768]{1,0:T(8,128)} %online-softmax.1, bf16[2048,768]{1,0:T(8,128)(2,1)} %param.60), kind=kOutput, calls=%fused_computation.284 | convolution fusion | flops 2422208512 | bytes 16916480 | tf_op jit(solution)/shard_map/dot_general | solution.py:17
  98.8 3.9 multiply_reduce_fusion
  102.7 3.7 subtract_multiply_fusion
  106.4 3.8 fusion.51
  110.2 2.9 convolution_convert_fusion.9
  113.2 1.6 convolution_convert_fusion.27
  114.8 1.5 multiply_reduce_fusion.11
  116.3 1.4 multiply_convert_fusion.5
  118.3 1.4 convolution_convert_fusion.13
  121.3 2.1 convolution_convert_fusion.8
  123.4 1.5 multiply_reduce_fusion.13
  125.4 1.5 copy-done.148
  128.3 3.1 convolution_convert_fusion.4
  131.4 1.8 multiply_reduce_fusion.14
  133.7 1.4 copy-done.40
  136.5 2.0 convolution_convert_fusion.24
  138.5 1.9 fusion.150
  140.3 4.8 %fusion.76 = bf16[8,256,32]{1,2,0:T(8,128)(2,1)} fusion(bf16[8,256,32]{1,2,0:T(8,128)(2,1)S(1)} %bitcast.221, f32[8,256,256]{1,2,0:T(8,128)} %fusion.150, f32[8,256,256]{1,2,0:T(8,128)} %get-tuple-element.215, f32[8,256]{1,0:T(8,128)S(1)} %copy-done.167), kind=kOutput, calls=%fused_computation.172 | convolution fusion | flops 37292288 | bytes 4464640 | tf_op jit(solution)/shard_map/dot_general | solution.py:492
  145.2 4.2 fusion.79
  149.4 2.3 convolution_convert_fusion.17
  151.7 1.5 fusion.151
  153.3 3.1 convolution_convert_fusion.3
  156.3 2.7 convolution_convert_fusion.2
  163.2 1.5 copy-done.152
  171.8 1.8 multiply_reduce_fusion.9
  175.3 1.5 convolution_convert_fusion.12
  176.8 3.4 convolution_convert_fusion.6
  181.5 1.7 fusion.64
  183.2 2.7 convolution_convert_fusion.5
  186.0 2.9 convolution_convert_fusion.7
  188.9 2.7 convolution_convert_fusion.1
  191.6 1.8 convolution_convert_fusion
  193.5 5.5 %convolution_convert_fusion.10 = bf16[768,1280]{1,0:T(8,128)(2,1)} fusion(bf16[2048,768]{1,0:T(8,128)(2,1)S(1)} %copy-done.46, bf16[2048,1280]{1,0:T(8,128)(2,1)S(1)} %convolution_convert_fusion), kind=kOutput, calls=%fused_computation.48 | convolution fusion | flops 4027514880 | bytes 10354688 | tf_op jit(solution)/shard_map/dot_general | solution.py:25
  199.0 6.2 %fusion.153 = f32[2048,768]{1,0:T(8,128)} fusion(bf16[2048,1280]{1,0:T(8,128)(2,1)S(1)} %convolution_convert_fusion, bf16[768,1280]{1,0:T(8,128)(2,1)S(1)} %copy-done.156), kind=kOutput, calls=%fused_computation.293 | convolution fusion | flops 4026531840 | bytes 13500416 | tf_op jit(solution)/shard_map/dot_general | solution.py:21
  205.3 1.8 convolution_convert_fusion.25
  207.3 4.7 %fusion.14 = (f32[768]{0:T(1024)S(1)}, f32[2048]{0:T(1024)S(1)}, f32[2048]{0:T(1024)S(1)}, f32[2048,768]{1,0:T(8,128)}) fusion(bf16[2048,768]{1,0:T(8,128)(2,1)S(1)} %copy-done.6, f32[2048]{0:T(1024)S(1)} %copy-done.87, f32[2048]{0:T(1024)S(1)} %copy-done.74, f32[768]{0:T(1024)S(1)} %copy-done.101, bf16[2048,256]{1,0:T(8,128)(2,1)S(1)} %copy-done.56, ...), kind=kOutput, calls=%fused_computation.25 | convolution fusion | flops 819457280 | bytes 10917888 | tf_op jit(solution)/shard_map/dot_general | solution.py:21
  212.0 3.1 convolution_convert_fusion.11
  215.3 2.9 fusion.36
  219.0 2.0 collective-permute-start.1
  221.3 4.0 convolution_convert_fusion.26
  225.4 8.4 %multiply_reduce_fusion.1 = (f32[768]{0:T(1024)S(1)}, f32[2048]{0:T(1024)S(1)}, f32[2048]{0:T(1024)S(1)}, f32[2048,768]{1,0:T(8,128)}) fusion(f32[2048,768]{1,0:T(8,128)} %copy-done.2, f32[2048]{0:T(1024)S(1)} %copy-done.81, f32[2048]{0:T(1024)S(1)} %copy-done.70, f32[768]{0:T(1024)S(1)} %copy-done.94, f32[2048,768]{1,0:T(8,128)} %fusion.153, ...), kind=kOutput, calls=%fused_computation.28 | convolution fusion | flops 819457280 | bytes 20355072 | tf_op jit(solution)/shard_map/dot_general | solution.py:21
  234.9 5.7 %multiply_convert_fusion = bf16[2048,768]{1,0:T(8,128)(2,1)S(1)} fusion(f32[2048,768]{1,0:T(8,128)} %get-tuple-element.236, f32[2048,768]{1,0:T(8,128)} %copy-done.2, f32[2048]{0:T(1024)S(1)} %broadcast_multiply_fusion, f32[2048]{0:T(1024)S(1)} %broadcast_multiply_fusion.1, f32[768]{0:T(1024)S(1)} %copy-done.94, f32[2048]{0:T(1024)S(1)} %copy-done.81, ...), kind=kLoop, calls=%fused_computation.29 | loop fusion | flops 12582912 | bytes 15764480 | tf_op jit(solution)/shard_map/convert_element_type | solution.py:602
  240.7 2.8 fusion.57
  246.0 3.6 fusion.13
  249.6 188.1 %shard_map.544 = (f32[40,1280]{1,0:T(8,128)}, f32[40,1280]{1,0:T(8,128)}, f32[40,1280]{1,0:T(8,128)}, f32[40,1280]{1,0:T(8,128)}, f32[40,1280]{1,0:T(8,128)}, /*...) custom-call(bf16[2,2,2,2,80,1280]{5,4,3,2,1,0:T(8,128)(2,1)} %bitcas, ...), custom_call_target="tpu_custom_call" | custom-call | tf_op jit(solution)/shard_map/pallas_call | solution.py:413
  439.1 1.4 slice_reduce_fusion
  440.5 1.5 fusion.137
  444.7 2.1 copy.96
  (489 shorter events, 75.1 us)
Async XLA Ops:
  0.7 71.7 %copy-start = (bf16[1280,1280]{1,0:T(8,128)(2,1)S(1)}, bf16[1280,1280]{1,0:T(8,128)(2,1)}, u32[]{:S(2)}) copy-start(bf16[1280,1280]{1,0:T(8,128)(2,1)} %param.55) | copy-start | bytes 9830404
  1.6 9.0 %copy-start.27 = (bf16[256,1280]{1,0:T(8,128)(2,1)S(1)}, bf16[256,1280]{1,0:T(8,128)(2,1)}, u32[]{:S(2)}) copy-start(bf16[256,1280]{1,0:T(8,128)(2,1)} %param.42) | copy-start | bytes 1966084
  1.6 16.7 %collective-permute-start = (s32[1024]{0:T(1024)S(1)}, s32[1024]{0:T(1024)S(1)}, u32[]{:S(2)}, u32[]{:S(2)}) collective-permute-start(s32[1024]{0:T(1024)S(1)} %bitcast.223), channel_id=1, source_target_pairs={{0,1},{1,0},{2,3},{3,2},{4,5},{5,4},{6,7},{7,6},{8,9},{9,8},{10,11... | collective-permute-start | bytes 12296 | tf_op jit(solution)/shard_map/ppermute | solution.py:444
  4.6 6.5 %copy-start.5 = (bf16[2048,768]{1,0:T(8,128)(2,1)S(1)}, bf16[2048,768]{1,0:T(8,128)(2,1)}, u32[]{:S(2)}) copy-start(bf16[2048,768]{1,0:T(8,128)(2,1)} %param.60) | copy-start | bytes 9437188
  10.5 85.6 %collective-permute-start.2 = (bf16[1024,262]{0,1:T(8,128)(2,1)}, bf16[1024,262]{0,1:T(8,128)(2,1)}, u32[]{:S(2)}, u32[]{:S(2)}) collective-permute-start(bf16[1024,262]{0,1:T(8,128)(2,1)} %bitcast.173), channel_id=1, source_target_pairs={{0,1},{1,0},{2,3},{3,2},{4,5},{5,4},{6,7},{7,6},{8,9},{9,8},{10,11... | collective-permute-start | bytes 1609736 | tf_op jit(solution)/shard_map/ppermute | solution.py:444
  10.7 5.5 %copy-start.124 = (f32[256]{0:T(256)}, f32[256]{0:T(256)S(1)}, u32[]{:S(2)}) copy-start(f32[256]{0:T(256)S(1)} %broadcast_multiply_fusion.23) | copy-start | bytes 3076
  11.0 5.2 %copy-start.133 = (f32[256]{0:T(256)}, f32[256]{0:T(256)S(1)}, u32[]{:S(2)}) copy-start(f32[256]{0:T(256)S(1)} %add_rsqrt_fusion.7) | copy-start | bytes 3076
  11.1 5.1 %copy-start.104 = (f32[1280]{0:T(1024)}, f32[1280]{0:T(1024)S(1)}, u32[]{:S(2)}) copy-start(f32[1280]{0:T(1024)S(1)} %convert_element_type.284) | copy-start | bytes 15364
  17.0 6.5 %copy-start.93 = (f32[768]{0:T(1024)}, f32[768]{0:T(1024)S(1)}, u32[]{:S(2)}) copy-start(f32[768]{0:T(1024)S(1)} %convert_element_type.288) | copy-start | bytes 9220
  17.6 32.5 %copy-start.88 = (f32[1280]{0:T(1024)}, f32[1280]{0:T(1024)S(1)}, u32[]{:S(2)}) copy-start(f32[1280]{0:T(1024)S(1)} %convert_element_type.294) | copy-start | bytes 15364
  18.3 4.3 copy-start.75
  28.9 6.8 %copy-start.38 = (bf16[2048,256]{1,0:T(8,128)(2,1)}, bf16[2048,256]{1,0:T(8,128)(2,1)S(1)}, u32[]{:S(2)}) copy-start(bf16[2048,256]{1,0:T(8,128)(2,1)S(1)} %convolution_convert_fusion.21) | copy-start | bytes 3145732
  36.3 9.7 %copy-start.120 = (f32[256]{0:T(256)}, f32[256]{0:T(256)S(1)}, u32[]{:S(2)}) copy-start(f32[256]{0:T(256)S(1)} %get-tuple-element.231) | copy-start | bytes 3076
  46.0 4.1 copy-start.153
  56.6 7.7 %copy-start.77 = (bf16[256,256]{0,1:T(8,128)(2,1)}, bf16[256,256]{0,1:T(8,128)(2,1)S(1)}, u32[]{:S(2)}) copy-start(bf16[256,256]{0,1:T(8,128)(2,1)S(1)} %convolution_convert_fusion.30) | copy-start | bytes 393220
  67.5 4.8 %copy-start.90 = (f32[1280]{0:T(1024)S(1)}, f32[1280]{0:T(1024)}, u32[]{:S(2)}) copy-start(f32[1280]{0:T(1024)} %convert_element_type.305) | copy-start | bytes 15364
  98.8 7.6 %slice-start.5 = ((s8[6291456]{0:T(1024)(128)(4,1)}), s8[4194304]{0:T(1024)(128)(4,1)S(1)}, s32[]{:S(2)}) async-start(s8[6291456]{0:T(1024)(128)(4,1)} %bitcast.186), calls=%async_computation.5 | async-start | bytes 8388608
  106.4 3.8 copy-start.13
  145.2 4.3 copy-start.12
  149.4 3.9 copy-start.20
  149.4 3.9 copy-start.58
  149.4 3.9 copy-start.118
  149.4 3.9 copy-start.130
  156.3 3.9 copy-start.59
  156.3 3.9 copy-start.150
  161.8 4.7 %copy-start.154 = (bf16[1280,1280]{1,0:T(8,128)(2,1)S(1)}, bf16[1280,1280]{1,0:T(8,128)(2,1)}, u32[]{:S(2)}) copy-start(bf16[1280,1280]{1,0:T(8,128)(2,1)} %param.47) | copy-start | bytes 9830404
  165.1 5.1 %slice-start = ((s8[10485760]{0:T(1024)(128)(4,1)}), s8[4194304]{0:T(1024)(128)(4,1)S(1)}, s32[]{:S(2)}) async-start(s8[10485760]{0:T(1024)(128)(4,1)} %bitcast.174), calls=%async_computation | async-start | bytes 8388608
  165.1 5.1 %slice-start.1 = ((s8[10485760]{0:T(1024)(128)(4,1)}), s8[4194304]{0:T(1024)(128)(4,1)S(1)}, s32[]{:S(2)}) async-start(s8[10485760]{0:T(1024)(128)(4,1)} %bitcast.174), calls=%async_computation.1 | async-start | bytes 8388608
  169.1 14.1 %copy-start.24 = (f32[256,1280]{1,0:T(8,128)}, f32[256,1280]{1,0:T(8,128)S(1)}, u32[]{:S(2)}) copy-start(f32[256,1280]{1,0:T(8,128)S(1)} %multiply_add_fusion.2) | copy-start | bytes 3932164
  193.5 5.5 %copy-start.156 = (bf16[768,1280]{1,0:T(8,128)(2,1)S(1)}, bf16[768,1280]{1,0:T(8,128)(2,1)}, u32[]{:S(2)}) copy-start(bf16[768,1280]{1,0:T(8,128)(2,1)} %param.41) | copy-start | bytes 5898244
  199.0 6.2 %copy-start.44 = (bf16[2048,768]{1,0:T(8,128)(2,1)S(1)}, bf16[2048,768]{1,0:T(8,128)(2,1)}, u32[]{:S(2)}) copy-start(bf16[2048,768]{1,0:T(8,128)(2,1)} %copy-done.43) | copy-start | bytes 9437188
  199.0 6.2 %copy-start.56 = (bf16[2048,256]{1,0:T(8,128)(2,1)S(1)}, bf16[2048,256]{1,0:T(8,128)(2,1)}, u32[]{:S(2)}) copy-start(bf16[2048,256]{1,0:T(8,128)(2,1)} %convolution_convert_fusion.13) | copy-start | bytes 3145732
  207.3 4.7 %copy-start.140 = (f32[768]{0:T(1024)S(1)}, f32[768]{0:T(1024)}, u32[]{:S(2)}) copy-start(f32[768]{0:T(1024)} %get-tuple-element.162) | copy-start | bytes 9220
  215.3 5.7 %copy-start.103 = (f32[1280]{0:T(1024)S(1)}, f32[1280]{0:T(1024)}, u32[]{:S(2)}) copy-start(f32[1280]{0:T(1024)} %get-tuple-element.171) | copy-start | bytes 15364
  215.3 5.8 %copy-start.132 = (f32[1280]{0:T(1024)S(1)}, f32[1280]{0:T(1024)}, u32[]{:S(2)}) copy-start(f32[1280]{0:T(1024)} %get-tuple-element.173) | copy-start | bytes 15364
  219.0 224.4 %collective-permute-start.1 = (bf16[1024,262]{0,1:T(8,128)(2,1)}, bf16[1024,262]{0,1:T(8,128)(2,1)}, u32[]{:S(2)}, u32[]{:S(2)}) collective-permute-start(bf16[1024,262]{0,1:T(8,128)(2,1)} %broadcast_select_fusion.2), channel_id=1, source_target_pairs={{0,1},{1,0},{2,3},{3,2},{4,5},{5,4},{6,7},{7,6},{8,9},{9,8},{10,11... | collective-permute-start | bytes 1609736 | tf_op jit(solution)/shard_map/ppermute | solution.py:444
  221.3 4.1 copy-start.70
  221.3 4.1 copy-start.81
  221.3 4.1 copy-start.94
  234.9 5.7 %copy-start.76 = (s32[2048]{0:T(1024)S(1)}, s32[2048]{0:T(1024)}, u32[]{:S(2)}) copy-start(s32[2048]{0:T(1024)} %copy-done.75) | copy-start | bytes 24580
  234.9 5.7 %copy-start.166 = (f32[768,384]{1,0:T(8,128)S(1)}, f32[768,384]{1,0:T(8,128)}, u32[]{:S(2)}) copy-start(f32[768,384]{1,0:T(8,128)} %fusion.36) | copy-start | bytes 3538948
  234.9 11.1 %slice-start.3 = ((s8[6291456]{0:T(1024)(128)(4,1)}), s8[4194304]{0:T(1024)(128)(4,1)S(1)}, s32[]{:S(2)}) async-start(s8[6291456]{0:T(1024)(128)(4,1)} %bitcast.178), calls=%async_computation.3 | async-start | bytes 8388608
  234.9 11.1 %slice-start.7 = ((s8[6291456]{0:T(1024)(128)(4,1)}), s8[4194304]{0:T(1024)(128)(4,1)S(1)}, s32[]{:S(2)}) async-start(s8[6291456]{0:T(1024)(128)(4,1)} %bitcast.188), calls=%async_computation.7 | async-start | bytes 8388608
  240.6 4.0 copy-start.54
  240.6 5.3 %slice-start.4 = ((s8[6291456]{0:T(1024)(128)(4,1)}), s8[2097152]{0:T(1024)(128)(4,1)S(1)}, s32[]{:S(2)}) async-start(s8[6291456]{0:T(1024)(128)(4,1)} %bitcast.178), calls=%async_computation.4 | async-start | bytes 4194304
  240.7 5.3 %slice-start.8 = ((s8[6291456]{0:T(1024)(128)(4,1)}), s8[2097152]{0:T(1024)(128)(4,1)S(1)}, s32[]{:S(2)}) async-start(s8[6291456]{0:T(1024)(128)(4,1)} %bitcast.188), calls=%async_computation.8 | async-start | bytes 4194304
  249.6 193.7 %copy-start.34 = (bf16[2048,262]{0,1:T(8,128)(2,1)S(1)}, bf16[2048,262]{0,1:T(8,128)(2,1)}, u32[]{:S(2)}) copy-start(bf16[2048,262]{0,1:T(8,128)(2,1)} %copy-done.33) | copy-start | bytes 3219460
  444.6 4.1 copy-start.99
  444.6 4.8 %copy-start.98 = (f32[40,256]{1,0:T(8,128)S(1)}, f32[40,256]{1,0:T(8,128)}, u32[]{:S(2)}) copy-start(f32[40,256]{1,0:T(8,128)} %get-tuple-element.279) | copy-start | bytes 122884
  444.6 5.4 %copy-start.68 = (f32[40,1280]{1,0:T(8,128)S(1)}, f32[40,1280]{1,0:T(8,128)}, u32[]{:S(2)}) copy-start(f32[40,1280]{1,0:T(8,128)} %get-tuple-element.280) | copy-start | bytes 614404
  444.7 6.0 %copy-start.67 = (f32[40,1280]{1,0:T(8,128)S(1)}, f32[40,1280]{1,0:T(8,128)}, u32[]{:S(2)}) copy-start(f32[40,1280]{1,0:T(8,128)} %get-tuple-element.282) | copy-start | bytes 614404
  444.7 6.7 %copy-start.66 = (f32[40,1280]{1,0:T(8,128)S(1)}, f32[40,1280]{1,0:T(8,128)}, u32[]{:S(2)}) copy-start(f32[40,1280]{1,0:T(8,128)} %get-tuple-element.283) | copy-start | bytes 614404
  444.7 7.4 %copy-start.97 = (f32[40,256]{1,0:T(8,128)S(1)}, f32[40,256]{1,0:T(8,128)}, u32[]{:S(2)}) copy-start(f32[40,256]{1,0:T(8,128)} %get-tuple-element.285) | copy-start | bytes 122884
  444.7 8.0 %copy-start.96 = (f32[40,256]{1,0:T(8,128)S(1)}, f32[40,256]{1,0:T(8,128)}, u32[]{:S(2)}) copy-start(f32[40,256]{1,0:T(8,128)} %get-tuple-element.286) | copy-start | bytes 122884
  444.7 8.6 %copy-start.65 = (f32[40,1280]{1,0:T(8,128)S(1)}, f32[40,1280]{1,0:T(8,128)}, u32[]{:S(2)}) copy-start(f32[40,1280]{1,0:T(8,128)} %get-tuple-element.287) | copy-start | bytes 614404
  444.7 9.3 %copy-start.64 = (f32[40,1280]{1,0:T(8,128)S(1)}, f32[40,1280]{1,0:T(8,128)}, u32[]{:S(2)}) copy-start(f32[40,1280]{1,0:T(8,128)} %get-tuple-element.288) | copy-start | bytes 614404
  446.8 7.9 %copy-start.63 = (f32[40,1280]{1,0:T(8,128)S(1)}, f32[40,1280]{1,0:T(8,128)}, u32[]{:S(2)}) copy-start(f32[40,1280]{1,0:T(8,128)} %get-tuple-element.290) | copy-start | bytes 614404
  446.8 8.6 %copy-start.62 = (f32[40,1280]{1,0:T(8,128)S(1)}, f32[40,1280]{1,0:T(8,128)}, u32[]{:S(2)}) copy-start(f32[40,1280]{1,0:T(8,128)} %get-tuple-element.291) | copy-start | bytes 614404
  446.8 9.2 %copy-start.95 = (f32[40,256]{1,0:T(8,128)S(1)}, f32[40,256]{1,0:T(8,128)}, u32[]{:S(2)}) copy-start(f32[40,256]{1,0:T(8,128)} %get-tuple-element.293) | copy-start | bytes 122884
  446.8 9.8 %copy-start.82 = (f32[40,768]{1,0:T(8,128)S(1)}, f32[40,768]{1,0:T(8,128)}, u32[]{:S(2)}) copy-start(f32[40,768]{1,0:T(8,128)} %get-tuple-element.294) | copy-start | bytes 368644
  447.5 9.8 %copy-start.71 = (f32[64,768]{1,0:T(8,128)S(1)}, f32[64,768]{1,0:T(8,128)}, u32[]{:S(2)}) copy-start(f32[64,768]{1,0:T(8,128)} %get-tuple-element.295) | copy-start | bytes 589828
  448.8 9.2 %copy-start.110 = (f32[24,256]{1,0:T(8,128)S(1)}, f32[24,256]{1,0:T(8,128)}, u32[]{:S(2)}) copy-start(f32[24,256]{1,0:T(8,128)} %get-tuple-element.297) | copy-start | bytes 73732
  448.8 9.8 %copy-start.92 = (f32[24,768]{1,0:T(8,128)S(1)}, f32[24,768]{1,0:T(8,128)}, u32[]{:S(2)}) copy-start(f32[24,768]{1,0:T(8,128)} %get-tuple-element.298) | copy-start | bytes 221188
  449.4 9.8 %copy-start.1 = (bf16[1280,1280]{1,0:T(8,128)(2,1)S(1)}, bf16[1280,1280]{1,0:T(8,128)(2,1)}, u32[]{:S(2)}) copy-start(bf16[1280,1280]{1,0:T(8,128)(2,1)} %param.55) | copy-start | bytes 9830404
  (116 other events, 241.2 us)
